TPU v7x, 32 devices: a whole 2x2x4 slice. The times are simulated.
32 devices in a mesh: row: 2 (over x), col: 4 (over y, core), head: 4 (over z).
Axes of the slice: x: 2, y: 2, z: 4, core: 2. Of those that a mesh axis runs over, the one named last changes fastest.
Arguments:
- tokens: bfloat16 [32, 128, 1024], P(('row', 'head'), 'col'), may hold values from -6 to 6
- valid: int32 [32, 128], P('row', 'col'), may hold values 0 or 1
- gain: float32 [1024], replicated, may hold values from 0.1 to 1.9
- w_qkv: bfloat16 [1024, 3, 1024], P(None, None, 'head'), may hold values from -0.1875 to 0.1875
- w_proj: bfloat16 [1024, 1024], P('head'), may hold values from -0.1875 to 0.1875
- rel_table: float32 [225, 16], P(None, 'head'), may hold values from -4 to 300
- cotangent: bfloat16 [32, 128, 1024], P(('row', 'head'), 'col'), may hold values from -6 to 6
Outputs:
- mixed: bfloat16 [32, 128, 1024], P(('row', 'head'), 'col')
- token_gradient: bfloat16 [32, 128, 1024], P(('row', 'head'), 'col')
- proj_grad: float32 [1024, 1024], P('head', ('row', 'col'))
- table_grad: float32 [225, 16], P(None, 'head')
All inputs are finite; a program needn't handle non-finite values. No bound on the sum of `valid` on one device may be relied on, other than what follows from the above.
Results may differ from a plain program's by a relative error of at most 0.0078.
Values may be sent and summed in bfloat16 or wider, within the bound.
A program may use at most 64 MiB of HBM per device.

v0:
```python
import math

import jax
import jax.numpy as jnp
from jax import lax
from jax.sharding import PartitionSpec as P

HD = 64
WIN = 8
SHIFT = 4


EPS = 1e-05
HIGH = lax.Precision.HIGHEST


def passed_along(value, axis, steps):
    count = lax.axis_size(axis)
    pairs = [(source, (source + steps) % count) for source in range(count)]
    return lax.ppermute(value, axis, pairs)


def region(index, grand_total):
    return jnp.where(
        index < grand_total - WIN, 0, jnp.where(index < grand_total - SHIFT, 1, 2)
    ).astype(jnp.int32)


def offsets():
    span = 2 * WIN - 1
    pos = jnp.arange(WIN * WIN, dtype=jnp.int32)
    prow = pos // WIN
    pcol = pos % WIN
    index = (prow[:, None] - prow[None, :] + WIN - 1) * span + (
        pcol[:, None] - pcol[None, :] + WIN - 1
    )
    table_ids = jnp.arange(span * span, dtype=jnp.int32)
    return (
        (index[:, :, None] == table_ids[None, None, :])
        .astype(jnp.float32)
        .reshape(WIN * WIN * WIN * WIN, span * span)
    )


def to_windows(block):
    nrow, ncol, heads, depth = block.shape
    block = block.reshape(nrow // WIN, WIN, ncol // WIN, WIN, heads, depth).transpose(
        0, 2, 4, 1, 3, 5
    )
    return block.reshape(nrow // WIN * (ncol // WIN), heads, WIN * WIN, depth)


def from_windows(block, nrow, ncol):
    count, heads, posn, depth = block.shape
    block = block.reshape(nrow // WIN, ncol // WIN, heads, WIN, WIN, depth).transpose(
        0, 3, 1, 4, 2, 5
    )
    return block.reshape(nrow, ncol, heads * depth)


def rows_in(block):
    return jnp.concatenate([block[SHIFT:], passed_along(block[:SHIFT], "row", -1)], 0)


def cols_in(block):
    return jnp.concatenate([block[:, SHIFT:], passed_along(block[:, :SHIFT], "col", -1)], 1)


def rows_out(block):
    return jnp.concatenate([passed_along(block[-SHIFT:], "row", 1), block[:-SHIFT]], 0)


def cols_out(block):
    return jnp.concatenate([passed_along(block[:, -SHIFT:], "col", 1), block[:, :-SHIFT]], 1)


def roll_in(block):
    return cols_in(rows_in(block))


def roll_out(block):
    return cols_out(rows_out(block))


def roll_pair(first, second, roller):
    return (roller(first), roller(second))


def head_sum(term_fn, part_rows):
    return lax.psum_scatter(
        term_fn(jnp.int32(0), lax.axis_size("head") * part_rows).astype(jnp.bfloat16),
        "head",
        scatter_dimension=0,
        tiled=True,
    ).astype(jnp.float32)


def attend(qkv, grad, labels, valid, bias, onehot):
    nrow, ncol = labels.shape
    feature_width = qkv.shape[3]
    heads = feature_width // HD
    scale = HD ** (-0.5)
    f32 = jnp.float32
    query = to_windows(qkv[:, :, 0].reshape(nrow, ncol, heads, HD))
    key = to_windows(qkv[:, :, 1].reshape(nrow, ncol, heads, HD))
    value = to_windows(qkv[:, :, 2].reshape(nrow, ncol, heads, HD))
    dout = to_windows(grad.reshape(nrow, ncol, heads, HD))
    lab_win = to_windows(labels[:, :, None, None])[:, 0, :, 0]
    val_win = to_windows(valid[:, :, None, None])[:, 0, :, 0]
    diagonal = jnp.eye(WIN * WIN, dtype=bool)
    allowed = (lab_win[:, :, None] == lab_win[:, None, :]) & (
        (val_win[:, None, :] == 1) | diagonal[None]
    )
    scores = (
        jnp.einsum("wiqd,wikd->wiqk", query, key, preferred_element_type=f32) * scale + bias[None]
    )
    scores = jnp.where(allowed[:, None], scores, -1e30)
    top = jnp.max(scores, -1, keepdims=True)
    expo = jnp.exp(scores - top)
    prob = expo / jnp.sum(expo, -1, keepdims=True)
    prob_b = prob.astype(jnp.bfloat16)
    attended = jnp.einsum("wiqk,wikd->wiqd", prob_b, value, preferred_element_type=f32).astype(
        jnp.bfloat16
    )
    dprob = jnp.einsum("wiqd,wikd->wiqk", dout, value, preferred_element_type=f32)
    dvalue = jnp.einsum("wiqk,wiqd->wikd", prob_b, dout, preferred_element_type=f32).astype(
        jnp.bfloat16
    )
    dscore = prob * (dprob - jnp.sum(prob * dprob, -1, keepdims=True))
    dscore_b = dscore.astype(jnp.bfloat16)
    dquery = (
        jnp.einsum("wiqk,wikd->wiqd", dscore_b, key, preferred_element_type=f32) * scale
    ).astype(jnp.bfloat16)
    dkey = (
        jnp.einsum("wiqk,wiqd->wikd", dscore_b, query, preferred_element_type=f32) * scale
    ).astype(jnp.bfloat16)
    summed = jnp.sum(dscore, 0).transpose(1, 2, 0).reshape(WIN * WIN * WIN * WIN, heads)
    tgrad = jnp.dot(onehot.T, summed, precision=HIGH)
    grads = jnp.stack(
        [
            from_windows(dquery, nrow, ncol),
            from_windows(dkey, nrow, ncol),
            from_windows(dvalue, nrow, ncol),
        ],
        2,
    )
    return (from_windows(attended, nrow, ncol), grads, tgrad)


def on_device(tokens, valid, gain, w_qkv, w_proj, rel_table, cotangent):
    part_rows, ncol, feature_width = tokens.shape
    tile_rows = part_rows * lax.axis_size("head")
    row_count = lax.axis_size("row")
    col_count = lax.axis_size("col")
    flat = tokens.astype(jnp.float32)
    token_average = jnp.mean(flat, -1, keepdims=True)
    centered_input = flat - token_average
    inverse_deviation = lax.rsqrt(
        jnp.mean(centered_input * centered_input, -1, keepdims=True) + EPS
    )
    standardized_input = centered_input * inverse_deviation
    normalized_tokens = (standardized_input * gain).astype(jnp.bfloat16)
    grad_tile = lax.all_gather(cotangent, "head", axis=0, tiled=True)
    out_grad = jnp.einsum(
        "rcd,nd->rcn", grad_tile, w_proj, preferred_element_type=jnp.float32
    ).astype(jnp.bfloat16)
    source = jnp.einsum(
        "rcd,dtn->rctn",
        lax.all_gather(normalized_tokens, "head", axis=0, tiled=True),
        w_qkv,
        preferred_element_type=jnp.float32,
    ).astype(jnp.bfloat16)
    rolled, rolled_grad = roll_pair(source, out_grad, roll_in)
    row_lab = region(
        lax.axis_index("row") * tile_rows + jnp.arange(tile_rows, dtype=jnp.int32),
        tile_rows * row_count,
    )
    col_lab = region(
        lax.axis_index("col") * ncol + jnp.arange(ncol, dtype=jnp.int32), ncol * col_count
    )
    labels = 3 * row_lab[:, None] + col_lab[None, :]
    onehot = offsets()
    heads = rel_table.shape[1]
    bias = (
        jnp.dot(onehot, rel_table, precision=HIGH)
        .reshape(WIN * WIN, WIN * WIN, heads)
        .transpose(2, 0, 1)
    )
    attended, grads, tgrad = attend(rolled, rolled_grad, labels, valid, bias, onehot)
    attn_out, qkv_grad = roll_pair(attended, grads, roll_out)

    def proj_term(start, count):
        return jnp.einsum("rcn,nd->rcd", attn_out, w_proj, preferred_element_type=jnp.float32)

    def back_term(start, count):
        return jnp.einsum("rctn,dtn->rcd", qkv_grad, w_qkv, preferred_element_type=jnp.float32)

    mixed = (flat + head_sum(proj_term, part_rows)).astype(jnp.bfloat16)
    norm_grad = head_sum(back_term, part_rows)
    scale = 1.0 / math.sqrt(tile_rows * ncol * row_count * col_count)
    weight_term = jnp.einsum("rcn,rcd->nd", attn_out, grad_tile, preferred_element_type=jnp.float32)
    proj_grad = (
        lax.psum_scatter(weight_term, ("row", "col"), scatter_dimension=1, tiled=True) * scale
    )
    table_grad = lax.psum(tgrad, ("row", "col")) * (WIN * scale)
    scaled_tokens = norm_grad * gain
    token_gradient = cotangent.astype(jnp.float32) + inverse_deviation * (
        scaled_tokens
        - jnp.mean(scaled_tokens, -1, keepdims=True)
        - standardized_input * jnp.mean(scaled_tokens * standardized_input, -1, keepdims=True)
    )
    return (mixed, token_gradient.astype(jnp.bfloat16), proj_grad, table_grad)


def solution(mesh):
    return jax.shard_map(
        on_device,
        mesh=mesh,
        in_specs=(
            P(("row", "head"), "col", None),
            P("row", "col"),
            P(),
            P(None, None, "head"),
            P("head", None),
            P(None, "head"),
            P(("row", "head"), "col", None),
        ),
        out_specs=(
            P(("row", "head"), "col", None),
            P(("row", "head"), "col", None),
            P("head", ("row", "col")),
            P(None, "head"),
        ),
        check_vma=False,
    )
```

profile of v0, /device:TPU:0, one launch (start us, length us, event | category | flops | bytes accessed | tf_op | source)
XLA Modules:
  0.0 211.9 jit_solution(7303914495705408818)
XLA Ops:
  10.9 1.9 fusion.29
  13.6 2.8 %fusion.17 = f32[4,64,64]{2,0,1:T(4,128)S(1)} fusion(s32[64,64]{1,0:T(8,128)S(1)} %add_add_fusion, f32[225,4]{0,1:T(4,128)S(1)} %copy-done.19), kind=kOutput, calls=%fused_computation.25 | convolution fusion | flops 45158400 | bytes 85520 | tf_op jit(solution)/shard_map/dot_general | solution.py:185
  17.7 22.6 %all-gather.5.cloned.1.call-done = bf16[16,32,1024]{2,1,0:T(8,128)(2,1)} async-done(((bf16[4,32,1024]{2,1,0:T(8,128)(2,1)}), bf16[16,32,1024]{2,1,0:T(8,128)(2,1)}) %all-gather.5.cloned.1.call-update) | async-done | bytes 1048592 | tf_op jit(solution)/shard_map/all_gather | solution.py:163
  40.3 1.7 convolution_convert_fusion.3
  43.5 26.3 %all-gather.3.cloned.1.call-done = bf16[16,32,1024]{2,1,0:T(8,128)(2,1)} async-done(((bf16[4,32,1024]{2,1,0:T(8,128)(2,1)}), bf16[16,32,1024]{2,1,0:T(8,128)(2,1)}) %all-gather.3.cloned.1.call-update) | async-done | bytes 1048592 | tf_op jit(solution)/shard_map/all_gather | solution.py:169
  69.9 2.2 %fusion.9 = bf16[16,32,3,256]{3,1,2,0:T(8,128)(2,1)S(1)} fusion(bf16[1024,3,256]{2,0,1:T(8,128)(2,1)S(1)} %copy-done, bf16[16,32,1024]{2,1,0:T(8,128)(2,1)} %all-gather.3.cloned.1.call-done), kind=kOutput, calls=%fused_computation.12 | convolution fusion | flops 805699584 | bytes 3407872 | tf_op jit(solution)/shard_map/rcd,dtn->rctn/dot_general | solution.py:167
  77.1 1.7 collective-permute-done
  79.4 2.0 collective-permute-done.1
  88.7 3.0 %convolution_convert_fusion.2 = bf16[8,4,64,64]{3,2,1,0:T(8,128)(2,1)} fusion(bf16[8,4,64,64]{3,2,1,0:T(8,128)(2,1)} %bitcast.104, f32[8,4,64]{2,1,0:T(4,128)S(1)} %get-tuple-element.13, f32[8,4,64,64]{2,3,1,0:T(8,128)} %copy-done.2), kind=kOutput, calls=%fused_computation.21 | convolution fusion | flops 17303616 | bytes 1056768 | tf_op jit(solution)/shard_map/wiqk,wikd->wiqd/dot_general | solution.py:122
  91.7 1.7 copy.46
  95.0 2.0 multiply_reduce_fusion
  100.0 2.9 %convolution_convert_fusion.1 = bf16[8,4,64,64]{3,2,1,0:T(8,128)(2,1)} fusion(bf16[8,4,64,64]{3,2,1,0:T(8,128)(2,1)} %bitcast.103, f32[8,4,64]{2,1,0:T(4,128)S(1)} %get-tuple-element.13, f32[8,4,64,64]{2,3,1,0:T(8,128)} %copy-done.2), kind=kOutput, calls=%fused_computation.20 | convolution fusion | flops 17303616 | bytes 1056768 | tf_op jit(solution)/shard_map/wiqk,wiqd->wikd/dot_general | solution.py:126
  103.0 2.5 %copy.55 = bf16[2,8,4,8,4,64]{5,4,3,2,1,0:T(4,128)(2,1)} copy(bf16[2,8,4,8,4,64]{5,3,1,4,2,0:T(8,128)(2,1)} %bitcast.106) | data formatting | bytes 524288 | tf_op jit(solution)/shard_map/transpose | solution.py:55
  105.5 2.2 %stack_reshape.11 = bf16[16,32,1,256]{3,1,2,0:T(8,128)(2,1)} reshape(bf16[2,8,4,8,4,64]{5,4,3,2,1,0:T(4,128)(2,1)} %copy.55) | data formatting | bytes 524288 | tf_op jit(solution)/shard_map/stack;reshape | solution.py:139
  107.7 2.8 %convolution_bitcast_fusion = f32[256,1024]{1,0:T(8,128)} fusion(bf16[16,32,1024]{2,1,0:T(8,128)(2,1)} %all-gather.5.cloned.1.call-done, bf16[12,32,256]{2,1,0:T(8,128)(2,1)S(1)} %slice.85, bf16[4,32,256]{2,1,0:T(8,128)(2,1)S(1)} %collective-permute-done.2, bf16[16,4,256]{2,1,0:T(4,128)(2,1)} %collective-permute-done.3), kind=kOutput, calls=%fused_computation.14 | convolution fusion | flops 269221888 | bytes 2392064 | tf_op jit(solution)/shard_map/rcn,rcd->nd/dot_general | solution.py:201
  114.7 2.2 %stack_reshape.10 = bf16[16,32,1,256]{3,1,2,0:T(8,128)(2,1)} reshape(bf16[2,8,4,8,4,64]{5,4,3,2,1,0:T(4,128)(2,1)} %copy.54) | data formatting | bytes 524288 | tf_op jit(solution)/shard_map/stack;reshape | solution.py:139
  119.4 6.7 %collective-permute-done.6 = bf16[4,32,3,256]{3,1,2,0:T(8,128)(2,1)S(1)} collective-permute-done((bf16[4,32,3,256]{3,1,2,0:T(8,128)(2,1)S(1)}, bf16[4,32,3,256]{3,1,2,0:T(8,128)(2,1)S(1)}, u32[]{:S(2)}, u32[]{:S(2)}) %collective-permute-start.6) | collective-permute-done | bytes 196640 | tf_op jit(solution)/shard_map/ppermute | solution.py:20
  126.2 4.0 %collective-permute-done.7 = bf16[16,4,3,256]{3,1,2,0:T(4,128)(2,1)S(1)} collective-permute-done((bf16[16,4,3,256]{3,1,2,0:T(4,128)(2,1)S(1)}, bf16[16,4,3,256]{3,1,2,0:T(4,128)(2,1)S(1)}, u32[]{:S(2)}, u32[]{:S(2)}) %collective-permute-start.7) | collective-permute-done | bytes 98336 | tf_op jit(solution)/shard_map/ppermute | solution.py:20
  130.2 2.0 bitcast_convert_fusion
  132.3 2.2 %convolution_convert_fusion = bf16[16,32,1024]{2,1,0:T(8,128)(2,1)} fusion(bf16[256,1024]{1,0:T(8,128)(2,1)S(1)} %copy-done.10, bf16[12,32,256]{2,1,0:T(8,128)(2,1)S(1)} %slice.85, bf16[4,32,256]{2,1,0:T(8,128)(2,1)S(1)} %collective-permute-done.2, bf16[16,4,256]{2,1,0:T(4,128)(2,1)} %collective-permute-done.3), kind=kOutput, calls=%fused_computation.11 | convolution fusion | flops 269746176 | bytes 1867776 | tf_op jit(solution)/shard_map/rcn,nd->rcd/dot_general | solution.py:193
  136.1 11.8 %psum.7 = f32[225,4]{0,1:T(4,128)S(1)} all-reduce(f32[225,4]{0,1:T(4,128)S(1)} %fusion.18), channel_id=1, replica_groups=mesh['row'=2,'col'=4,'head'=4] {'row','col'}, use_global_device_ids=true, to_apply=%region_11.12 | all-reduce | flops 900 | bytes 7200 | tf_op jit(solution)/shard_map/psum | solution.py:205
  150.1 25.1 %reduce-scatter.6.cloned.1.call-done = bf16[4,32,1024]{2,1,0:T(8,128)(2,1)} async-done(((bf16[16,32,1024]{2,1,0:T(8,128)(2,1)}), bf16[4,32,1024]{2,1,0:T(8,128)(2,1)}) %reduce-scatter.6.cloned.1.call-update) | async-done | bytes 262160 | tf_op jit(solution)/shard_map/reduce_scatter | solution.py:90
  176.4 26.9 %reduce-scatter.4.cloned.1.call-done = bf16[4,32,1024]{2,1,0:T(8,128)(2,1)} async-done(((bf16[16,32,1024]{2,1,0:T(8,128)(2,1)}), bf16[4,32,1024]{2,1,0:T(8,128)(2,1)}) %reduce-scatter.4.cloned.1.call-update) | async-done | bytes 262160 | tf_op jit(solution)/shard_map/reduce_scatter | solution.py:90
  203.3 2.1 fusion.34
  (125 shorter events, 36.4 us)
Async XLA Ops:
  7.2 62.7 %copy-start = (bf16[1024,3,256]{2,0,1:T(8,128)(2,1)S(1)}, bf16[1024,3,256]{2,0,1:T(8,128)(2,1)}, u32[]{:S(2)}) copy-start(bf16[1024,3,256]{2,0,1:T(8,128)(2,1)} %param.10) | copy-start | bytes 4718596
  7.2 6.4 %copy-start.19 = (f32[225,4]{0,1:T(4,128)S(1)}, f32[225,4]{0,1:T(4,128)}, u32[]{:S(2)}) copy-start(f32[225,4]{0,1:T(4,128)} %param.12) | copy-start | bytes 10804
  7.2 9.5 %copy-start.18 = (s32[16,32]{1,0:T(8,128)S(1)}, s32[16,32]{1,0:T(8,128)}, u32[]{:S(2)}) copy-start(s32[16,32]{1,0:T(8,128)} %param.8) | copy-start | bytes 6148
  7.2 33.1 %all-gather.5.cloned.1.call-start = ((), (), s32[]{:S(2)}) async-start(), calls=%async_computation.5 | async-start | bytes 1310720 | tf_op jit(solution)/shard_map/all_gather | solution.py:163
  7.9 32.4 %copy-start.9 = (bf16[256,1024]{1,0:T(8,128)(2,1)S(1)}, bf16[256,1024]{1,0:T(8,128)(2,1)}, u32[]{:S(2)}) copy-start(bf16[256,1024]{1,0:T(8,128)(2,1)} %param.11) | copy-start | bytes 1572868
  7.9 61.9 %all-gather.3.cloned.1.call-start = ((), (), s32[]{:S(2)}) async-start(), calls=%async_computation.3 | async-start | bytes 1310720 | tf_op jit(solution)/shard_map/all_gather | solution.py:169
  12.8 135.7 %reduce-scatter.8.cloned.1.call-start = ((), (), s32[]{:S(2)}) async-start(), calls=%async_computation.7 | async-start | bytes 1179648 | tf_op jit(solution)/shard_map/reduce_scatter | solution.py:203
  42.0 31.7 %collective-permute-start.4 = (bf16[4,32,256]{2,1,0:T(8,128)(2,1)S(1)}, bf16[4,32,256]{2,1,0:T(8,128)(2,1)S(1)}, u32[]{:S(2)}, u32[]{:S(2)}) collective-permute-start(bf16[4,32,256]{2,1,0:T(8,128)(2,1)S(1)} %slice.87), channel_id=1, source_target_pairs={{0,16},{16,0},{1,17},{17,1},{2,18},{18,2},{3,19},{19,3},{4,20},{20... | collective-permute-start | bytes 196616 | tf_op jit(solution)/shard_map/ppermute | solution.py:20
  72.2 6.6 %collective-permute-start = (bf16[4,32,3,256]{3,1,2,0:T(8,128)(2,1)S(1)}, bf16[4,32,3,256]{3,1,2,0:T(8,128)(2,1)S(1)}, u32[]{:S(2)}, u32[]{:S(2)}) collective-permute-start(bf16[4,32,3,256]{3,1,2,0:T(8,128)(2,1)S(1)} %slice.77), channel_id=1, source_target_pairs={{0,16},{16,0},{1,17},{17,1},{2,18},{18,2},{3,19},{19,3},{4,20},{20... | collective-permute-start | bytes 589832 | tf_op jit(solution)/shard_map/ppermute | solution.py:20
  73.7 2.1 %collective-permute-start.5 = (bf16[16,4,256]{2,1,0:T(4,128)(2,1)S(1)}, bf16[16,4,256]{2,1,0:T(4,128)(2,1)S(1)}, u32[]{:S(2)}, u32[]{:S(2)}) collective-permute-start(bf16[16,4,256]{2,1,0:T(4,128)(2,1)S(1)} %pad_maximum_fusion.6), channel_id=1, source_target_pairs={{0,12},{4,0},{8,4},{12,8},{1,13},{5,1},{9,5},{13,9},{2,14},{6,2},{... | collective-permute-start | bytes 98312 | tf_op jit(solution)/shard_map/ppermute | solution.py:20
  78.8 2.7 %collective-permute-start.1 = (bf16[16,4,3,256]{3,1,2,0:T(4,128)(2,1)S(1)}, bf16[16,4,3,256]{3,1,2,0:T(4,128)(2,1)S(1)}, u32[]{:S(2)}, u32[]{:S(2)}) collective-permute-start(bf16[16,4,3,256]{3,1,2,0:T(4,128)(2,1)S(1)} %pad_maximum_fusion.5), channel_id=1, source_target_pairs={{0,12},{4,0},{8,4},{12,8},{1,13},{5,1},{9,5},{13,9},{2,14},{6,2},{... | collective-permute-start | bytes 294920 | tf_op jit(solution)/shard_map/ppermute | solution.py:20
  93.8 3.2 %copy-start.4 = (bf16[16,32,256]{2,1,0:T(8,128)(2,1)}, bf16[16,32,256]{2,1,0:T(8,128)(2,1)S(1)}, u32[]{:S(2)}) copy-start(bf16[16,32,256]{2,1,0:T(8,128)(2,1)S(1)} %reshape.236) | copy-start | bytes 786436
  93.8 4.7 %collective-permute-start.2 = (bf16[4,32,256]{2,1,0:T(8,128)(2,1)S(1)}, bf16[4,32,256]{2,1,0:T(8,128)(2,1)S(1)}, u32[]{:S(2)}, u32[]{:S(2)}) collective-permute-start(bf16[4,32,256]{2,1,0:T(8,128)(2,1)S(1)} %slice.84), channel_id=1, source_target_pairs={{0,16},{16,0},{1,17},{17,1},{2,18},{18,2},{3,19},{19,3},{4,20},{20... | collective-permute-start | bytes 196616 | tf_op jit(solution)/shard_map/ppermute | solution.py:20
  99.2 8.5 %collective-permute-start.3 = (bf16[16,4,256]{2,1,0:T(4,128)(2,1)}, bf16[16,4,256]{2,1,0:T(4,128)(2,1)}, u32[]{:S(2)}, u32[]{:S(2)}) collective-permute-start(bf16[16,4,256]{2,1,0:T(4,128)(2,1)} %pad_maximum_fusion.7), channel_id=1, source_target_pairs={{0,4},{4,8},{8,12},{12,0},{1,5},{5,9},{9,13},{13,1},{2,6},{6,10},{... | collective-permute-start | bytes 98312 | tf_op jit(solution)/shard_map/ppermute | solution.py:20
  110.4 64.7 %reduce-scatter.6.cloned.1.call-start = ((), (), s32[]{:S(2)}) async-start(), calls=%async_computation.6 | async-start | bytes 1310720 | tf_op jit(solution)/shard_map/reduce_scatter | solution.py:90
  118.7 7.4 %collective-permute-start.6 = (bf16[4,32,3,256]{3,1,2,0:T(8,128)(2,1)S(1)}, bf16[4,32,3,256]{3,1,2,0:T(8,128)(2,1)S(1)}, u32[]{:S(2)}, u32[]{:S(2)}) collective-permute-start(bf16[4,32,3,256]{3,1,2,0:T(8,128)(2,1)S(1)} %slice.90), channel_id=1, source_target_pairs={{0,16},{16,0},{1,17},{17,1},{2,18},{18,2},{3,19},{19,3},{4,20},{20... | collective-permute-start | bytes 589832 | tf_op jit(solution)/shard_map/ppermute | solution.py:20
  126.1 6.2 %copy-start.10 = (bf16[256,1024]{1,0:T(8,128)(2,1)S(1)}, bf16[256,1024]{1,0:T(8,128)(2,1)}, u32[]{:S(2)}) copy-start(bf16[256,1024]{1,0:T(8,128)(2,1)} %param.11) | copy-start | bytes 1572868
  126.1 4.1 %collective-permute-start.7 = (bf16[16,4,3,256]{3,1,2,0:T(4,128)(2,1)S(1)}, bf16[16,4,3,256]{3,1,2,0:T(4,128)(2,1)S(1)}, u32[]{:S(2)}, u32[]{:S(2)}) collective-permute-start(bf16[16,4,3,256]{3,1,2,0:T(4,128)(2,1)S(1)} %pad_maximum_fusion.4), channel_id=1, source_target_pairs={{0,4},{4,8},{8,12},{12,0},{1,5},{5,9},{9,13},{13,1},{2,6},{6,10},{... | collective-permute-start | bytes 294920 | tf_op jit(solution)/shard_map/ppermute | solution.py:20
  132.3 71.0 %reduce-scatter.4.cloned.1.call-start = ((), (), s32[]{:S(2)}) async-start(), calls=%async_computation.4 | async-start | bytes 1310720 | tf_op jit(solution)/shard_map/reduce_scatter | solution.py:90
  134.5 40.7 %copy-start.1 = (bf16[4,32,1024]{2,1,0:T(8,128)(2,1)S(1)}, bf16[4,32,1024]{2,1,0:T(8,128)(2,1)}, u32[]{:S(2)}) copy-start(bf16[4,32,1024]{2,1,0:T(8,128)(2,1)} %param.7) | copy-start | bytes 786436
  134.5 40.7 %copy-start.12 = (f32[4,32]{1,0:T(4,128)S(1)}, f32[4,32]{1,0:T(4,128)}, u32[]{:S(2)}) copy-start(f32[4,32]{1,0:T(4,128)} %copy-done.11) | copy-start | bytes 1540
  134.5 40.7 %copy-start.13 = (f32[1024]{0:T(1024)S(1)}, f32[1024]{0:T(1024)}, u32[]{:S(2)}) copy-start(f32[1024]{0:T(1024)} %param.9) | copy-start | bytes 12292
  134.5 40.7 %copy-start.15 = (f32[4,32]{1,0:T(4,128)S(1)}, f32[4,32]{1,0:T(4,128)}, u32[]{:S(2)}) copy-start(f32[4,32]{1,0:T(4,128)} %copy-done.14) | copy-start | bytes 1540
  134.5 68.7 %copy-start.8 = (bf16[4,32,1024]{2,1,0:T(8,128)(2,1)S(1)}, bf16[4,32,1024]{2,1,0:T(8,128)(2,1)}, u32[]{:S(2)}) copy-start(bf16[4,32,1024]{2,1,0:T(8,128)(2,1)} %param.13) | copy-start | bytes 786436
  (9 other events, 11.3 us)
Sparse Core Ops, SparseCore 0:
  9.6 30.6 all-gather.4
  42.4 27.3 all-gather.2
  110.6 35.2 reduce-scatter.7
  148.0 27.1 reduce-scatter.5
  177.4 25.8 reduce-scatter.3
where the time goes:
time: 213 us; the launch traced here: 212 us
  waiting for transfers between devices  118 us (55%)
  matrix products  25.9 us (12%)
  local copies, waits for them, and re-layouts  20.6 us (10%)
  between operations  14.3 us (7%)
  other arithmetic  14.1 us (7%)
  blocking collectives  11.8 us (6%)
  starting transfers between devices  7.12 us (3%)
    reduce_scatter x2, waiting for transfers between devices, head_sum(): lax.psum_scatter(term_fn(jnp.int32(0), lax.axis_size('head') * part_rows)...  52 us
    all_gather x1, waiting for transfers between devices, on_device(): lax.all_gather(normalized_tokens, 'head', axis=0, tiled=True)  26.3 us
    all_gather x1, waiting for transfers between devices, on_device(): grad_tile = lax.all_gather(cotangent, 'head', axis=0, tiled=True)  22.6 us
    ppermute x8, waiting for transfers between devices, passed_along(): return lax.ppermute(value, axis, pairs)  16.4 us
    psum x1, blocking collectives, on_device(): table_grad = lax.psum(tgrad, ('row', 'col')) * (WIN * scale)  11.8 us
    ppermute x8, starting transfers between devices, passed_along(): return lax.ppermute(value, axis, pairs)  6.74 us
    transpose x4, local copies, waits for them, and re-layouts, from_windows(): block.reshape(nrow // WIN, ncol // WIN, heads, WIN, WIN, depth)  6.41 us
    another operation x4, local copies, waits for them, and re-layouts, attend(): jnp.stack([from_windows(dquery, nrow, ncol), from_windows(dkey, nrow, nco...  4.68 us
  transfers between devices with their start and end apart: 13, of which 10 were waited for; matrix products, arithmetic and copies ran while one was open for 19% of the time, Pallas kernels for 0%

commit v1 on v0

v1 whole, which is shorter than its diff:
```python
import functools
import math

import jax
import jax.numpy as jnp
from jax import lax
from jax.experimental import pallas as pl
from jax.experimental.pallas import tpu as pltpu
from jax.sharding import PartitionSpec as P

HD = 64
WIN = 8
SHIFT = 4
UNIT = SHIFT * SHIFT
EPS = 1e-05
HIGH = lax.Precision.HIGHEST
MESH = pl.DeviceIdType.MESH
F32 = jnp.float32
BF16 = jnp.bfloat16
NN = (((1,), (0,)), ((), ()))
NT = (((1,), (1,)), ((), ()))
TN = (((0,), (0,)), ((), ()))


def dot(a, b, dims):
    return lax.dot_general(a, b, dims, preferred_element_type=F32)


def region(index, grand_total):
    return jnp.where(
        index < grand_total - WIN, 0, jnp.where(index < grand_total - SHIFT, 1, 2)
    ).astype(jnp.int32)


def window_places():
    pos = jnp.arange(WIN * WIN, dtype=jnp.int32)
    prow = pos // 32 * SHIFT + pos // SHIFT % SHIFT
    pcol = pos // 16 % 2 * SHIFT + pos % SHIFT
    return prow, pcol


def offsets():
    span = 2 * WIN - 1
    prow, pcol = window_places()
    index = (prow[:, None] - prow[None, :] + WIN - 1) * span + (
        pcol[:, None] - pcol[None, :] + WIN - 1
    )
    table_ids = jnp.arange(span * span, dtype=jnp.int32)
    return (
        (index[:, :, None] == table_ids[None, None, :])
        .astype(F32)
        .reshape(WIN * WIN * WIN * WIN, span * span)
    )


def to_units(block):
    nrow, ncol, width = block.shape
    block = block.reshape(nrow, ncol // SHIFT, SHIFT, width).transpose(1, 0, 2, 3)
    return block.reshape(nrow * ncol, width)


def from_units(block, nrow, ncol):
    width = block.shape[-1]
    block = block.reshape(ncol // SHIFT, nrow, SHIFT, width).transpose(1, 0, 2, 3)
    return block.reshape(nrow, ncol, width)


def kernel(
    sizes,
    tok_ref, cot_ref, gain_ref, wq_ref, wp_ref, bias_ref, mask_ref,
    mixed_ref, tg_ref, pg_ref, ts_ref,
    xhat, rstd, gath, tile, back, terms, recv, wsend, wrecv, tsend, trecv, tsum,
    ag_send, ag_recv, in_send, in_recv, out_send, out_recv, rs_send, rs_recv,
    pl_send, pl_recv,
):
    n, nr, nc, plane, direct = sizes
    h = lax.axis_index("head")
    r = lax.axis_index("row")
    c = lax.axis_index("col")
    part, width = tok_ref.shape
    group = wp_ref.shape[0]
    ucols = part // UNIT

    def at(dr, dc):
        return {"row": lax.rem(r + dr % nr, nr), "col": lax.rem(c + dc % nc, nc)}

    barrier = pltpu.get_barrier_semaphore()
    for dr, dc in plane:
        pl.semaphore_signal(barrier, inc=1, device_id=at(dr, dc), device_id_type=MESH)

    for dh in (1, n - 1):
        pl.semaphore_signal(
            barrier, inc=1, device_id={"head": lax.rem(h + dh, n)}, device_id_type=MESH
        )
    gath[0, h] = cot_ref[...]
    pl.semaphore_wait(barrier, len(plane) + 2)

    def ag_copy(arr, way, t, blk):
        step = 1 - 2 * way
        return pltpu.make_async_remote_copy(
            src_ref=gath.at[arr, blk], dst_ref=gath.at[arr, blk],
            send_sem=ag_send.at[arr, way, t], recv_sem=ag_recv.at[arr, way, t],
            device_id={"head": h + step}, device_id_type=MESH,
        )

    def sends(way, t):
        if way == 0:
            return (h < n - 1) & (h >= t)
        return (h > 0) & (h < n - t)

    def receives(way, t):
        return h > t if way == 0 else h < n - 1 - t

    def ag_send_step(arr, way, t):
        @pl.when(sends(way, t))
        def _():
            ag_copy(arr, way, t, h - (1 - 2 * way) * t).start()

    for way in range(2):
        ag_send_step(0, way, 0)

    x = tok_ref[...].astype(F32)
    cen = x - jnp.mean(x, -1, keepdims=True)
    inv = lax.rsqrt(jnp.mean(cen * cen, -1, keepdims=True) + EPS)
    std = cen * inv
    xhat[...] = std
    rstd[...] = inv
    gath[1, h] = (std * gain_ref[...]).astype(BF16)
    for way in range(2):
        ag_send_step(1, way, 0)

    def in_copy(k):
        if k == 0:
            src, dst, dev = tile.at[0, pl.ds(1, ucols - 1)], tile.at[n, pl.ds(1, ucols - 1)], at(-1, 0)
        elif k == n:
            src, dst, dev = tile.at[0, 0], tile.at[n, ucols], at(-1, -1)
        else:
            src, dst, dev = tile.at[k, 0], tile.at[k, ucols], at(0, -1)
        return pltpu.make_async_remote_copy(
            src_ref=src, dst_ref=dst, send_sem=in_send.at[k], recv_sem=in_recv.at[k],
            device_id=dev, device_id_type=MESH,
        )

    def project(blk):
        g = dot(gath[0, blk], wp_ref[...], NT).astype(BF16)
        q = dot(gath[1, blk], wq_ref[...], NN).astype(BF16)
        tile[blk, pl.ds(0, ucols), :, pl.ds(0, 3 * group)] = q.reshape(ucols, UNIT, 3 * group)
        tile[blk, pl.ds(0, ucols), :, pl.ds(3 * group, group)] = g.reshape(ucols, UNIT, group)
        for k in range(n):
            @pl.when(blk == k)
            def _():
                in_copy(k).start()
                if k == 0:
                    in_copy(n).start()

    project(h)
    for t in range(n - 1):
        for arr in range(2):
            for way in range(2):
                @pl.when(receives(way, t))
                def _():
                    step = 1 - 2 * way
                    pltpu.make_async_remote_copy(
                        src_ref=gath.at[arr, h - step * (t + 1)],
                        dst_ref=gath.at[arr, h - step * (t + 1)],
                        send_sem=ag_send.at[arr, way, t], recv_sem=ag_recv.at[arr, way, t],
                        device_id={"head": h - step}, device_id_type=MESH,
                    ).wait_recv()
                if t + 1 < n - 1:
                    ag_send_step(arr, way, t + 1)
        for way in range(2):
            @pl.when(receives(way, t))
            def _():
                project(h - (1 - 2 * way) * (t + 1))
    for k in range(n + 1):
        in_copy(k).wait_recv()

    lane = lax.broadcasted_iota(jnp.int32, (2 * WIN * WIN, 2 * HD), 1)
    first = lane < HD
    keep0 = jnp.where(first, 1.0, 0.0).astype(BF16)
    keep1 = jnp.where(first, 0.0, 1.0).astype(BF16)
    half = 2 * WIN * WIN
    scale = HD ** (-0.5)
    tsum[...] = jnp.zeros_like(tsum)

    def pair_step(i, jp):
        def places():
            return [(2 * i + 1 + ur, 4 * jp + 1 + 2 * w) for w in range(2) for ur in range(2)]

        def load(at_lane):
            return jnp.concatenate(
                [tile[ur, pl.ds(uc, 2), :, pl.ds(at_lane, 2 * HD)].reshape(2 * UNIT, 2 * HD) for ur, uc in places()], 0
            )

        def save(value, at_lane):
            for k, (ur, uc) in enumerate(places()):
                back[ur, pl.ds(uc, 2), :, pl.ds(at_lane, 2 * HD)] = (
                    value[2 * UNIT * k : 2 * UNIT * (k + 1)].astype(BF16).reshape(2, UNIT, 2 * HD)
                )

        for hp in range(group // (2 * HD)):
            base = hp * 2 * HD
            q, k, v, do = [load(base + s * group) for s in range(4)]
            qs = jnp.concatenate([q * keep0, q * keep1], 0)
            dos = jnp.concatenate([do * keep0, do * keep1], 0)
            m = mask_ref[2 * i + jp]
            s = dot(qs, k, NT) * scale + bias_ref[hp] + jnp.concatenate([m, m], 0)
            e = jnp.exp(s - jnp.max(s, -1, keepdims=True))
            p = e / jnp.sum(e, -1, keepdims=True)
            pb = p.astype(BF16)
            att = dot(pb, v, NN)
            save(jnp.where(first, att[:half], att[half:]), base)
            dp = dot(dos, v, NT)
            save(dot(pb, dos, TN), base + 3 * group)
            ds = p * (dp - jnp.sum(p * dp, -1, keepdims=True))
            dsb = ds.astype(BF16)
            dq = dot(dsb, k, NN) * scale
            save(jnp.where(first, dq[:half], dq[half:]), base + group)
            save(dot(dsb, qs, TN) * scale, base + 2 * group)
            tsum[hp] += ds

    def out_copy(k):
        if k == 0:
            src, dst, dev = back.at[n, pl.ds(1, ucols - 1)], back.at[0, pl.ds(1, ucols - 1)], at(1, 0)
        elif k == 1:
            src, dst, dev = back.at[n, ucols], back.at[0, 0], at(1, 1)
        else:
            src, dst, dev = back.at[k - 1, ucols], back.at[k - 1, 0], at(0, 1)
        return pltpu.make_async_remote_copy(
            src_ref=src, dst_ref=dst, send_sem=out_send.at[k], recv_sem=out_recv.at[k],
            device_id=dev, device_id_type=MESH,
        )

    for i in range(n // 2 - 1, -1, -1):
        for jp in range(ucols // 4):
            pair_step(i, jp)
        if i == n // 2 - 1:
            out_copy(0).start()
            out_copy(1).start()
    for k in range(1, n):
        out_copy(k + 1).start()

    low = lax.broadcasted_iota(jnp.int32, (WIN * WIN, 2 * HD), 1) < HD
    for hp in range(group // (2 * HD)):
        folds = []
        for k in range(2):
            f = tsum[hp, k * half : k * half + HD] + tsum[hp, k * half + HD : (k + 1) * half]
            folds.append(f + pltpu.roll(f, HD, 1))
        tsend[hp] = jnp.where(low, folds[0], folds[1])

    for k in range(n + 1):
        out_copy(k).wait_recv()

    def block(d, start, count):
        return back[d, pl.ds(0, ucols), :, pl.ds(start, count)].reshape(part, count)

    def rs_copy(arr, way, d):
        step = 1 - 2 * way
        return pltpu.make_async_remote_copy(
            src_ref=terms.at[arr, d], dst_ref=recv.at[arr, way, d],
            send_sem=rs_send.at[arr, way, d], recv_sem=rs_recv.at[arr, way, d],
            device_id={"head": h + step}, device_id_type=MESH,
        )

    def rs_arrived(arr, way, d):
        step = 1 - 2 * way
        pltpu.make_async_remote_copy(
            src_ref=terms.at[arr, d], dst_ref=recv.at[arr, way, d],
            send_sem=rs_send.at[arr, way, d], recv_sem=rs_recv.at[arr, way, d],
            device_id={"head": h - step}, device_id_type=MESH,
        ).wait_recv()

    order = []
    for k in range(n // 2):
        order += [n - 1 - k, k]
    for arr in range(2):
        for d in order:
            if arr == 0:
                term = dot(block(d, 0, group), wp_ref[...], NN)
            else:
                term = dot(block(d, group, 3 * group), wq_ref[...], NT)
            terms[arr, d] = term.astype(BF16)
            if d > 0:
                @pl.when(h == 0)
                def _():
                    rs_copy(arr, 0, d).start()
            if d < n - 1:
                @pl.when(h == n - 1)
                def _():
                    rs_copy(arr, 1, d).start()

    def pl_copy(kind, o):
        dr, dc = plane[o]
        there = at(dr, dc)
        if kind == 0:
            src, dst = wsend.at[there["row"] * nc + there["col"]], wrecv.at[o]
        else:
            src, dst = tsend, trecv.at[o]
        return pltpu.make_async_remote_copy(
            src_ref=src, dst_ref=dst, send_sem=pl_send.at[kind, o], recv_sem=pl_recv.at[kind, o],
            device_id=there, device_id_type=MESH,
        )

    attn = jnp.concatenate([block(d, 0, group) for d in range(n)], 0)
    grad = gath[0].reshape(n * part, width)
    wterm = dot(attn, grad, TN)
    if direct:
        piece = width // (nr * nc)
        for j in range(nr * nc):
            wsend[j] = wterm[:, j * piece : (j + 1) * piece].astype(BF16)
        for o in range(len(plane)):
            for kind in range(2):
                pl_copy(kind, o).start()
    else:
        pg_ref[...] = wterm
        ts_ref[...] = tsend[...]

    for arr in range(2):
        for d in order:
            if d > 1:
                @pl.when((h > 0) & (h < d))
                def _():
                    rs_arrived(arr, 0, d)
                    terms[arr, d] = (terms[arr, d].astype(F32) + recv[arr, 0, d].astype(F32)).astype(BF16)
                    rs_copy(arr, 0, d).start()
            if d < n - 2:
                @pl.when((h > d) & (h < n - 1))
                def _():
                    rs_arrived(arr, 1, d)
                    terms[arr, d] = (terms[arr, d].astype(F32) + recv[arr, 1, d].astype(F32)).astype(BF16)
                    rs_copy(arr, 1, d).start()

    def total(arr):
        xhat2 = terms.at[arr, h]
        sides = [h > 0, h < n - 1]
        for way in range(2):
            @pl.when(sides[way])
            def _():
                rs_arrived(arr, way, h)

            @pl.when(jnp.logical_not(sides[way]))
            def _():
                recv[arr, way, h] = jnp.zeros((part, width), BF16)
        return xhat2[...].astype(F32) + recv[arr, 0, h].astype(F32) + recv[arr, 1, h].astype(F32)

    mixed_ref[...] = (tok_ref[...].astype(F32) + total(0)).astype(BF16)
    gg = total(1) * gain_ref[...]
    std = xhat[...]
    tg_ref[...] = (
        cot_ref[...].astype(F32)
        + rstd[...]
        * (
            gg
            - jnp.mean(gg, -1, keepdims=True)
            - std * jnp.mean(gg * std, -1, keepdims=True)
        )
    ).astype(BF16)

    if direct:
        for o in range(len(plane)):
            for kind in range(2):
                pl_copy(kind, o).wait_recv()
        wsum = wsend[r * nc + c].astype(F32)
        tall = tsend[...]
        for o in range(len(plane)):
            wsum = wsum + wrecv[o].astype(F32)
            tall = tall + trecv[o]
        pg_ref[...] = wsum
        ts_ref[...] = tall
        for o in range(len(plane)):
            for kind in range(2):
                pl_copy(kind, o).wait_send()

    for arr in range(2):
        for way in range(2):
            for t in range(n - 1):
                @pl.when(sends(way, t))
                def _():
                    ag_copy(arr, way, t, h - (1 - 2 * way) * t).wait_send()
    for k in range(n + 1):
        in_copy(k).wait_send()
        out_copy(k).wait_send()
    for arr in range(2):
        for d in range(n):
            if d > 0:
                @pl.when(h < d)
                def _():
                    rs_copy(arr, 0, d).wait_send()
            if d < n - 1:
                @pl.when(h > d)
                def _():
                    rs_copy(arr, 1, d).wait_send()


def on_device(n, nr, nc, tokens, valid, gain, w_qkv, w_proj, rel_table, cotangent):
    part_rows, ncol, width = tokens.shape
    tile_rows = part_rows * n
    part = part_rows * ncol
    heads = rel_table.shape[1]
    group = heads * HD
    pairs = heads // 2
    pos = WIN * WIN
    ucols = ncol // SHIFT

    row_lab = region(
        lax.axis_index("row") * tile_rows + jnp.arange(tile_rows, dtype=jnp.int32), tile_rows * nr
    )
    col_lab = region(lax.axis_index("col") * ncol + jnp.arange(ncol, dtype=jnp.int32), ncol * nc)
    labels = 3 * row_lab[:, None] + col_lab[None, :]

    def to_pairs(block):
        block = block.reshape(tile_rows // WIN, 2, SHIFT, ncol // WIN, 2, SHIFT)
        return block.transpose(0, 3, 1, 4, 2, 5).reshape(-1, 2 * pos)

    lab = to_pairs(labels) + 16 * (jnp.arange(2 * pos, dtype=jnp.int32) // pos)[None]
    val = to_pairs(valid)
    allowed = (lab[:, :, None] == lab[:, None, :]) & (
        (val[:, None, :] == 1) | jnp.eye(2 * pos, dtype=bool)[None]
    )
    mask = jnp.where(allowed, 0.0, -1e30).astype(F32)
    onehot = offsets()
    bias = jnp.dot(onehot, rel_table, precision=HIGH).reshape(pos, pos, heads).transpose(2, 0, 1)
    bias = jnp.broadcast_to(
        bias.reshape(pairs, 2, 1, pos, 1, pos), (pairs, 2, 2, pos, 2, pos)
    ).reshape(pairs, 4 * pos, 2 * pos)

    direct = nr * nc <= 8
    if direct:
        plane = [(dr, dc) for dr in range(nr) for dc in range(nc) if (dr, dc) != (0, 0)]
    else:
        six = [(1, 0), (nr - 1, 0), (0, 1), (0, nc - 1), (1, 1), (nr - 1, nc - 1)]
        plane = sorted(set(six))
    count = len(plane)
    piece = width // (nr * nc)
    vmem = pl.BlockSpec(memory_space=pltpu.VMEM)
    dma = pltpu.SemaphoreType.DMA
    mixed, token_gradient, wsum, tall = pl.pallas_call(
        functools.partial(kernel, (n, nr, nc, tuple(plane), direct)),
        out_shape=(
            jax.ShapeDtypeStruct((part, width), BF16),
            jax.ShapeDtypeStruct((part, width), BF16),
            jax.ShapeDtypeStruct((group, piece if direct else width), F32),
            jax.ShapeDtypeStruct((pairs, pos, 2 * HD), F32),
        ),
        in_specs=[vmem] * 7,
        out_specs=[vmem] * 4,
        scratch_shapes=[
            pltpu.VMEM((part, width), F32),
            pltpu.VMEM((part, 1), F32),
            pltpu.VMEM((2, n, part, width), BF16),
            pltpu.VMEM((n + 1, ucols + 1, UNIT, 4 * group), BF16),
            pltpu.VMEM((n + 1, ucols + 1, UNIT, 4 * group), BF16),
            pltpu.VMEM((2, n, part, width), BF16),
            pltpu.VMEM((2, 2, n, part, width), BF16),
            pltpu.VMEM((nr * nc, group, piece) if direct else (1, 16, 128), BF16),
            pltpu.VMEM((count, group, piece) if direct else (1, 16, 128), BF16),
            pltpu.VMEM((pairs, pos, 2 * HD), F32),
            pltpu.VMEM((count, pairs, pos, 2 * HD) if direct else (1, 16, 128), F32),
            pltpu.VMEM((pairs, 4 * pos, 2 * pos), F32),
            dma((2, 2, n)),
            dma((2, 2, n)),
            dma((n + 1,)),
            dma((n + 1,)),
            dma((n + 1,)),
            dma((n + 1,)),
            dma((2, 2, n)),
            dma((2, 2, n)),
            dma((2, count)),
            dma((2, count)),
        ],
        compiler_params=pltpu.CompilerParams(
            collective_id=0, has_side_effects=True, vmem_limit_bytes=48 * 1024 * 1024
        ),
    )(
        to_units(tokens),
        to_units(cotangent),
        gain[None],
        w_qkv.reshape(width, 3 * group),
        w_proj,
        bias,
        mask,
    )
    if not direct:
        wsum = lax.psum_scatter(wsum, ("row", "col"), scatter_dimension=1, tiled=True)
        tall = lax.psum(tall, ("row", "col"))
    scale = 1.0 / math.sqrt(tile_rows * ncol * nr * nc)
    summed = tall.reshape(pairs, pos, 2, pos).transpose(1, 3, 0, 2).reshape(pos * pos, heads)
    table_grad = jnp.dot(onehot.T, summed, precision=HIGH) * (WIN * scale)
    return (
        from_units(mixed, part_rows, ncol),
        from_units(token_gradient, part_rows, ncol),
        wsum * scale,
        table_grad,
    )


def solution(mesh):
    n, nr, nc = (mesh.shape[name] for name in ("head", "row", "col"))
    return jax.shard_map(
        functools.partial(on_device, n, nr, nc),
        mesh=mesh,
        in_specs=(
            P(("row", "head"), "col", None),
            P("row", "col"),
            P(),
            P(None, None, "head"),
            P("head", None),
            P(None, "head"),
            P(("row", "head"), "col", None),
        ),
        out_specs=(
            P(("row", "head"), "col", None),
            P(("row", "head"), "col", None),
            P("head", ("row", "col")),
            P(None, "head"),
        ),
        check_vma=False,
    )
```

time: 213 us -> 116 us (0.54)
  the two profiles are of different devices: /device:TPU:0 before, /device:TPU:12 now
where the time goes in v1:
time: 116 us
  Pallas kernels  99.6 us (86%)
  local copies, waits for them, and re-layouts  9.23 us (8%)
  matrix products  4.83 us (4%)
    pallas_call x1, Pallas kernels, on_device(): pl.pallas_call(functools.partial(kernel, (n, nr, nc, tuple(plane), direct...  99.6 us
    dot_general x1, matrix products, on_device(): jnp.dot(onehot, rel_table, precision=HIGH).reshape(pos, pos, heads)  2.82 us
    unnamed x17, local copies, waits for them, and re-layouts  2.42 us

profile of v1, /device:TPU:12, one launch (start us, length us, event | category | flops | bytes accessed | tf_op | source)
XLA Modules:
  0.0 115.6 jit_solution(959731975900572613)
XLA Ops:
  0.7 1.2 %reshape.359 = bf16[4,8,4,1024]{3,2,1,0:T(4,128)(2,1)S(1)} reshape(bf16[4,32,1024]{2,1,0:T(8,128)(2,1)} %param.7) | data formatting | bytes 524288 | tf_op jit(solution)/shard_map/reshape | solution.py:58
  1.9 0.1 copy.39
  2.0 0.1 reshape.361
  2.2 0.1 copy.38
  2.3 1.8 %copy.28 = bf16[1024,3,256]{0,2,1:T(8,128)(2,1)} copy(bf16[1024,3,256]{2,0,1:T(8,128)(2,1)S(1)} %copy-done.5) | data formatting | bytes 3145728 | tf_op args[3]
  4.1 1.7 %copy.31.wq_ref = bf16[1024,768]{1,0:T(8,128)(2,1)S(1)} copy(bf16[1024,768]{0,1:T(8,128)(2,1)} %bitcast.26) | data formatting | bytes 3145728 | tf_op jit(solution)/shard_map/reshape | solution.py:478
  6.0 2.8 %fusion = f32[64,64,4]{1,2,0:T(4,128)S(1)} fusion(s32[64,64]{1,0:T(8,128)S(1)} %add_add_fusion, f32[225,4]{0,1:T(4,128)S(1)} %copy-done), kind=kOutput, calls=%fused_computation.2 | convolution fusion | flops 45158400 | bytes 85520 | tf_op jit(solution)/shard_map/dot_general | solution.py:422
  8.8 0.1 broadcast_in_dim.56
  9.0 0.3 reshape.364.bias_ref
  9.4 0.1 add.209
  9.6 0.1 eq.73
  9.7 0.1 eq.75
  9.8 0.1 and_select_fusion.mask_ref
  10.0 99.6 %shard_map.102 = (bf16[128,1024]{1,0:T(8,128)(2,1)S(1)}, bf16[128,1024]{1,0:T(8,128)(2,1)S(1)}, f32[256,128]{1,0:T(8,128)S(1)}, f32[2,64,128]{2,1,0:T(8,128)S(1)}) custom-call(bf16[128,1024]{1,0:T(8,128)(2,1)S(1)} %reshape.360.tok_ref, bf16[128,1024]{1,0:T(8,128)(2,1)S(1)} %reshape.362.cot_ref, f32[1,1024]{1,0:T(1,128)S(1)} %bitcast.25, ...), custom_call_target="tpu_custom_call" | custom-call | tf_op jit(solution)/shard_map/pallas_call | solution.py:437
  109.6 0.6 copy-done.2
  110.2 0.1 reshape.365
  110.4 0.8 reshape.366
  111.2 0.1 reshape.367
  111.3 0.1 copy.33
  111.4 0.8 reshape.368
  112.2 0.7 broadcast_multiply_fusion
  112.8 0.1 reshape.369
  113.0 0.1 reshape.370
  113.6 2.0 %fusion.4 = f32[225,4]{0,1:T(4,128)} fusion(f32[4096,4]{0,1:T(4,128)S(1)} %reshape.370, s32[4096]{0:T(1024)S(1)} %add_add_fusion.1), kind=kOutput, calls=%fused_computation.6 | convolution fusion | flops 45159300 | bytes 85520 | tf_op jit(solution)/shard_map/dot_general | solution.py:488
  (39 shorter events, 1.0 us)
Async XLA Ops:
  0.6 5.3 %copy-start = (f32[225,4]{0,1:T(4,128)S(1)}, f32[225,4]{0,1:T(4,128)}, u32[]{:S(2)}) copy-start(f32[225,4]{0,1:T(4,128)} %param.12) | copy-start | bytes 10804
  0.6 1.4 %copy-start.6 = (bf16[4,32,1024]{2,1,0:T(8,128)(2,1)S(1)}, bf16[4,32,1024]{2,1,0:T(8,128)(2,1)}, u32[]{:S(2)}) copy-start(bf16[4,32,1024]{2,1,0:T(8,128)(2,1)} %param.13) | copy-start | bytes 786436
  0.7 1.7 %copy-start.5 = (bf16[1024,3,256]{2,0,1:T(8,128)(2,1)S(1)}, bf16[1024,3,256]{2,0,1:T(8,128)(2,1)}, u32[]{:S(2)}) copy-start(bf16[1024,3,256]{2,0,1:T(8,128)(2,1)} %param.10) | copy-start | bytes 4718596
  5.8 3.7 %copy-start.7 = (s32[16,32]{1,0:T(8,128)S(1)}, s32[16,32]{1,0:T(8,128)}, u32[]{:S(2)}) copy-start(s32[16,32]{1,0:T(8,128)} %param.8) | copy-start | bytes 6148
  5.9 4.0 %copy-start.1 = (bf16[256,1024]{1,0:T(8,128)(2,1)S(1)}, bf16[256,1024]{1,0:T(8,128)(2,1)}, u32[]{:S(2)}) copy-start(bf16[256,1024]{1,0:T(8,128)(2,1)} %wp_ref.1) | copy-start | bytes 1572868
  6.0 4.0 %copy-start.4 = (f32[1024]{0:T(1024)S(1)}, f32[1024]{0:T(1024)}, u32[]{:S(2)}) copy-start(f32[1024]{0:T(1024)} %param.9) | copy-start | bytes 12292
  109.6 0.6 copy-start.2
  110.3 2.5 %copy-start.3 = (f32[2,64,128]{2,1,0:T(8,128)S(1)}, f32[2,64,128]{2,1,0:T(8,128)}, u32[]{:S(2)}) copy-start(f32[2,64,128]{2,1,0:T(8,128)} %copy-done.2) | copy-start | bytes 196612

commit v2 on v1

v2 whole, which is shorter than its diff:
```python
import functools
import math

import jax
import jax.numpy as jnp
from jax import lax
from jax.experimental import pallas as pl
from jax.experimental.pallas import tpu as pltpu
from jax.sharding import PartitionSpec as P

HD = 64
WIN = 8
SHIFT = 4
UNIT = SHIFT * SHIFT
EPS = 1e-05
HIGH = lax.Precision.HIGHEST
MESH = pl.DeviceIdType.MESH
F32 = jnp.float32
BF16 = jnp.bfloat16
NN = (((1,), (0,)), ((), ()))
NT = (((1,), (1,)), ((), ()))
TN = (((0,), (0,)), ((), ()))


def dot(a, b, dims):
    return lax.dot_general(a, b, dims, preferred_element_type=F32)


def region(index, grand_total):
    return jnp.where(
        index < grand_total - WIN, 0, jnp.where(index < grand_total - SHIFT, 1, 2)
    ).astype(jnp.int32)


def window_places():
    pos = jnp.arange(WIN * WIN, dtype=jnp.int32)
    prow = pos // 32 * SHIFT + pos // SHIFT % SHIFT
    pcol = pos // 16 % 2 * SHIFT + pos % SHIFT
    return prow, pcol


def offsets():
    span = 2 * WIN - 1
    prow, pcol = window_places()
    index = (prow[:, None] - prow[None, :] + WIN - 1) * span + (
        pcol[:, None] - pcol[None, :] + WIN - 1
    )
    table_ids = jnp.arange(span * span, dtype=jnp.int32)
    return (
        (index[:, :, None] == table_ids[None, None, :])
        .astype(F32)
        .reshape(WIN * WIN * WIN * WIN, span * span)
    )


def kernel(
    sizes,
    tok_ref, cot_ref, gain_ref, wq_ref, wp_ref, bias_ref, mask_ref,
    mixed_ref, tg_ref, pg_ref, ts_ref,
    xhat, rstd, gath, tile_q, tile_g, back_a, back_d, probs, terms, recv, wsend, wrecv, tsend, trecv, tsum,
    ag_send, ag_recv, in_send, in_recv, out_send, out_recv, rs_send, rs_recv,
    pl_send, pl_recv,
):
    n, nr, nc, plane, direct, ncol, pg_scale = sizes
    h = lax.axis_index("head")
    r = lax.axis_index("row")
    c = lax.axis_index("col")
    part, width = tok_ref.shape
    group = wp_ref.shape[0]
    ucols = part // UNIT
    COT, NORM = 0, 1

    def at(dr, dc):
        return {"row": lax.rem(r + dr % nr, nr), "col": lax.rem(c + dc % nc, nc)}

    barrier = pltpu.get_barrier_semaphore()
    for dr, dc in plane:
        pl.semaphore_signal(barrier, inc=1, device_id=at(dr, dc), device_id_type=MESH)
    for dh in (1, n - 1):
        pl.semaphore_signal(
            barrier, inc=1, device_id={"head": lax.rem(h + dh, n)}, device_id_type=MESH
        )

    unit_at = lax.broadcasted_iota(jnp.int32, (part, part), 0)
    patch_at = lax.broadcasted_iota(jnp.int32, (part, part), 1)
    wanted = unit_at // SHIFT % SHIFT * ncol + unit_at // UNIT * SHIFT + unit_at % SHIFT
    perm = jnp.where(wanted == patch_at, 1.0, 0.0).astype(BF16)

    x = dot(perm, tok_ref[...], NN)
    cen = x - jnp.mean(x, -1, keepdims=True)
    inv = lax.rsqrt(jnp.mean(cen * cen, -1, keepdims=True) + EPS)
    std = cen * inv
    xhat[...] = std
    rstd[...] = inv
    gath[NORM, h] = (std * gain_ref[...]).astype(BF16)
    gath[COT, h] = dot(perm, cot_ref[...], NN).astype(BF16)
    pl.semaphore_wait(barrier, len(plane) + 2)

    def ag_copy(arr, way, t, blk):
        step = 1 - 2 * way
        return pltpu.make_async_remote_copy(
            src_ref=gath.at[arr, blk], dst_ref=gath.at[arr, blk],
            send_sem=ag_send.at[arr, way, t], recv_sem=ag_recv.at[arr, way, t],
            device_id={"head": h + step}, device_id_type=MESH,
        )

    def sends(way, t):
        if way == 0:
            return (h < n - 1) & (h >= t)
        return (h > 0) & (h < n - t)

    def receives(way, t):
        return h > t if way == 0 else h < n - 1 - t

    def ag_send_step(arr, way, t):
        @pl.when(sends(way, t))
        def _():
            ag_copy(arr, way, t, h - (1 - 2 * way) * t).start()

    def ag_receive_step(arr, way, t):
        @pl.when(receives(way, t))
        def _():
            step = 1 - 2 * way
            pltpu.make_async_remote_copy(
                src_ref=gath.at[arr, h - step * (t + 1)],
                dst_ref=gath.at[arr, h - step * (t + 1)],
                send_sem=ag_send.at[arr, way, t], recv_sem=ag_recv.at[arr, way, t],
                device_id={"head": h - step}, device_id_type=MESH,
            ).wait_recv()
        if t + 1 < n - 1:
            ag_send_step(arr, way, t + 1)

    def cot_after(t):
        @pl.when((h == t) & (h < n - 1))
        def _():
            ag_copy(COT, 0, 0, h).start()

        @pl.when((h == n - 1 - t) & (h > 0))
        def _():
            ag_copy(COT, 1, 0, h).start()

    def in_copy(kind, k):
        tile = (tile_q, tile_g)[kind]
        if k == 0:
            src, dst, dev = tile.at[0, pl.ds(1, ucols - 1)], tile.at[n, pl.ds(1, ucols - 1)], at(-1, 0)
        elif k == n:
            src, dst, dev = tile.at[0, 0], tile.at[n, ucols], at(-1, -1)
        else:
            src, dst, dev = tile.at[k, 0], tile.at[k, ucols], at(0, -1)
        return pltpu.make_async_remote_copy(
            src_ref=src, dst_ref=dst, send_sem=in_send.at[kind, k], recv_sem=in_recv.at[kind, k],
            device_id=dev, device_id_type=MESH,
        )

    def project(kind, blk):
        if kind == 0:
            for s in range(3):
                out = dot(gath[NORM, blk], wq_ref[s], NN).astype(BF16)
                tile_q[blk, pl.ds(0, ucols), :, pl.ds(s * group, group)] = out.reshape(
                    ucols, UNIT, group
                )
        else:
            out = dot(gath[COT, blk], wp_ref[...], NT).astype(BF16)
            tile_g[blk, pl.ds(0, ucols)] = out.reshape(ucols, UNIT, group)
        for k in range(n):
            @pl.when(blk == k)
            def _():
                in_copy(kind, k).start()
                if k == 0:
                    in_copy(kind, n).start()

    def project_step(kind, t):
        for way in range(2):
            @pl.when(receives(way, t))
            def _():
                project(kind, h - (1 - 2 * way) * (t + 1))

    for way in range(2):
        ag_send_step(NORM, way, 0)
    cot_after(0)
    project(0, h)
    for t in range(n - 1):
        for way in range(2):
            ag_receive_step(NORM, way, t)
        cot_after(t + 1)
        project_step(0, t)
    project(1, h)
    for way in range(2):
        ag_receive_step(COT, way, 0)
    project_step(1, 0)
    for k in range(n + 1):
        in_copy(0, k).wait_recv()

    lane = lax.broadcasted_iota(jnp.int32, (2 * WIN * WIN, 2 * HD), 1)
    first = lane < HD
    keep0 = jnp.where(first, 1.0, 0.0).astype(BF16)
    keep1 = jnp.where(first, 0.0, 1.0).astype(BF16)
    half = 2 * WIN * WIN
    scale = HD ** (-0.5)
    heads2 = group // (2 * HD)
    pairs2 = ucols // 4

    def places(i, jp):
        return [(2 * i + 1 + ur, 4 * jp + 1 + 2 * w) for w in range(2) for ur in range(2)]

    def load(tile, i, jp, at_lane):
        return jnp.concatenate(
            [
                tile[ur, pl.ds(uc, 2), :, pl.ds(at_lane, 2 * HD)].reshape(2 * UNIT, 2 * HD)
                for ur, uc in places(i, jp)
            ],
            0,
        )

    def save(tile, i, jp, at_lane, value):
        for k, (ur, uc) in enumerate(places(i, jp)):
            tile[ur, pl.ds(uc, 2), :, pl.ds(at_lane, 2 * HD)] = (
                value[2 * UNIT * k : 2 * UNIT * (k + 1)].astype(BF16).reshape(2, UNIT, 2 * HD)
            )

    def both(value):
        return jnp.concatenate([value * keep0, value * keep1], 0)

    def chosen(value):
        return jnp.where(first, value[:half], value[half:])

    def forward(i, jp):
        for hp in range(heads2):
            base = hp * 2 * HD
            q, k, v = [load(tile_q, i, jp, base + s * group) for s in range(3)]
            m = mask_ref[pairs2 * i + jp]
            s = dot(both(q), k, NT) * scale + bias_ref[hp] + jnp.concatenate([m, m], 0)
            e = jnp.exp(s - jnp.max(s, -1, keepdims=True))
            p = e / jnp.sum(e, -1, keepdims=True)
            probs[pairs2 * i + jp, hp] = p
            save(back_a, i, jp, base, chosen(dot(p.astype(BF16), v, NN)))

    def backward(i, jp):
        for hp in range(heads2):
            base = hp * 2 * HD
            q, k, v = [load(tile_q, i, jp, base + s * group) for s in range(3)]
            dos = both(load(tile_g, i, jp, base))
            p = probs[pairs2 * i + jp, hp]
            dp = dot(dos, v, NT)
            save(back_d, i, jp, base + 2 * group, dot(p.astype(BF16), dos, TN))
            ds = p * (dp - jnp.sum(p * dp, -1, keepdims=True))
            dsb = ds.astype(BF16)
            save(back_d, i, jp, base, chosen(dot(dsb, k, NN) * scale))
            save(back_d, i, jp, base + group, dot(dsb, both(q), TN) * scale)
            tsum[hp] += ds

    def out_copy(kind, k):
        back = (back_a, back_d)[kind]
        if k == 0:
            src, dst, dev = back.at[n, pl.ds(1, ucols - 1)], back.at[0, pl.ds(1, ucols - 1)], at(1, 0)
        elif k == n:
            src, dst, dev = back.at[n, ucols], back.at[0, 0], at(1, 1)
        else:
            src, dst, dev = back.at[k, ucols], back.at[k, 0], at(0, 1)
        return pltpu.make_async_remote_copy(
            src_ref=src, dst_ref=dst, send_sem=out_send.at[kind, k], recv_sem=out_recv.at[kind, k],
            device_id=dev, device_id_type=MESH,
        )

    def windows(kind, step, between):
        for i in range(n // 2 - 1, -1, -1):
            for jp in range(pairs2 - 1, -1, -1):
                step(i, jp)
                if jp == pairs2 - 1:
                    for k in (2 * i + 1, 2 * i + 2):
                        out_copy(kind, k if k < n else n).start()
            if i == n // 2 - 1:
                out_copy(kind, 0).start()
            between(i)

    def between_forward(i):
        if i == n // 2 - 1:
            for t in range(1, n - 2):
                for way in range(2):
                    ag_receive_step(COT, way, t)

    windows(0, forward, between_forward)
    for t in range(1, n - 2):
        project_step(1, t)
    for k in range(n + 1):
        out_copy(0, k).wait_recv()

    def block(back, d):
        return back[d, pl.ds(0, ucols)].reshape(part, back.shape[-1])

    def rs_copy(arr, way, d):
        step = 1 - 2 * way
        return pltpu.make_async_remote_copy(
            src_ref=terms.at[arr, d], dst_ref=recv.at[arr, way, d],
            send_sem=rs_send.at[arr, way, d], recv_sem=rs_recv.at[arr, way, d],
            device_id={"head": h + step}, device_id_type=MESH,
        )

    def rs_arrived(arr, way, d):
        step = 1 - 2 * way
        pltpu.make_async_remote_copy(
            src_ref=terms.at[arr, d], dst_ref=recv.at[arr, way, d],
            send_sem=rs_send.at[arr, way, d], recv_sem=rs_recv.at[arr, way, d],
            device_id={"head": h - step}, device_id_type=MESH,
        ).wait_recv()

    order = []
    for k in range(n // 2):
        order += [n - 1 - k, k]

    def rs_start(arr):
        for d in order:
            if arr == 0:
                term = dot(block(back_a, d), wp_ref[...], NN)
            else:
                grads = block(back_d, d)
                term = sum(
                    dot(grads[:, s * group : (s + 1) * group], wq_ref[s], NT) for s in range(3)
                )
            terms[arr, d] = term.astype(BF16)
            if d > 0:
                @pl.when(h == 0)
                def _():
                    rs_copy(arr, 0, d).start()
            if d < n - 1:
                @pl.when(h == n - 1)
                def _():
                    rs_copy(arr, 1, d).start()

    def pass_on(arr, way, d):
        rs_arrived(arr, way, d)
        terms[arr, d] = (terms[arr, d].astype(F32) + recv[arr, way, d].astype(F32)).astype(BF16)
        rs_copy(arr, way, d).start()

    def rs_transit(arr, d):
        if d > 1:
            @pl.when((h > 0) & (h < d))
            def _():
                pass_on(arr, 0, d)
        if d < n - 2:
            @pl.when((h > d) & (h < n - 1))
            def _():
                pass_on(arr, 1, d)

    def total(arr):
        sides = [h > 0, h < n - 1]
        for way in range(2):
            @pl.when(sides[way])
            def _():
                rs_arrived(arr, way, h)

            @pl.when(jnp.logical_not(sides[way]))
            def _():
                recv[arr, way, h] = jnp.zeros((part, width), BF16)
        return (
            terms[arr, h].astype(F32) + recv[arr, 0, h].astype(F32) + recv[arr, 1, h].astype(F32)
        )

    rs_start(0)
    for way in range(2):
        ag_receive_step(COT, way, n - 2)
    project_step(1, n - 2)
    for k in range(n + 1):
        in_copy(1, k).wait_recv()

    def between_backward(i):
        for d in order[: n // 2] if i == n // 2 - 1 else order[n // 2 :]:
            rs_transit(0, d)

    tsum[...] = jnp.zeros_like(tsum)
    windows(1, backward, between_backward)

    low = lax.broadcasted_iota(jnp.int32, (WIN * WIN, 2 * HD), 1) < HD
    for hp in range(heads2):
        folds = []
        for k in range(2):
            f = tsum[hp, k * half : k * half + HD] + tsum[hp, k * half + HD : (k + 1) * half]
            folds.append(f + pltpu.roll(f, HD, 1))
        tsend[hp] = jnp.where(low, folds[0], folds[1])

    for k in range(n + 1):
        out_copy(1, k).wait_recv()
    rs_start(1)

    def pl_copy(kind, o):
        dr, dc = plane[o]
        there = at(dr, dc)
        if kind == 0:
            src, dst = wsend.at[there["row"] * nc + there["col"]], wrecv.at[o]
        else:
            src, dst = tsend, trecv.at[o]
        return pltpu.make_async_remote_copy(
            src_ref=src, dst_ref=dst, send_sem=pl_send.at[kind, o], recv_sem=pl_recv.at[kind, o],
            device_id=there, device_id_type=MESH,
        )

    attn = jnp.concatenate([block(back_a, d) for d in range(n)], 0)
    wterm = dot(attn, gath[COT].reshape(n * part, width), TN)
    if direct:
        piece = width // (nr * nc)
        for j in range(nr * nc):
            wsend[j] = wterm[:, j * piece : (j + 1) * piece].astype(BF16)
        for o in range(len(plane)):
            for kind in range(2):
                pl_copy(kind, o).start()
    else:
        pg_ref[...] = wterm
        ts_ref[...] = tsend[...]

    for d in order:
        rs_transit(1, d)

    mixed = dot(perm, tok_ref[...], NN) + total(0)
    mixed_ref[...] = dot(perm, mixed.astype(BF16), TN).astype(BF16)

    if direct:
        for o in range(len(plane)):
            for kind in range(2):
                pl_copy(kind, o).wait_recv()
        wsum = wsend[r * nc + c].astype(F32)
        tall = tsend[...]
        for o in range(len(plane)):
            wsum = wsum + wrecv[o].astype(F32)
            tall = tall + trecv[o]
        pg_ref[...] = wsum * pg_scale
        ts_ref[...] = tall
        for o in range(len(plane)):
            for kind in range(2):
                pl_copy(kind, o).wait_send()

    gg = total(1) * gain_ref[...]
    std = xhat[...]
    tg = gath[COT, h].astype(F32) + rstd[...] * (
        gg - jnp.mean(gg, -1, keepdims=True) - std * jnp.mean(gg * std, -1, keepdims=True)
    )
    tg_ref[...] = dot(perm, tg.astype(BF16), TN).astype(BF16)

    for arr in range(2):
        for way in range(2):
            for t in range(n - 1):
                @pl.when(sends(way, t))
                def _():
                    ag_copy(arr, way, t, h - (1 - 2 * way) * t).wait_send()
    for kind in range(2):
        for k in range(n + 1):
            in_copy(kind, k).wait_send()
            out_copy(kind, k).wait_send()
    for arr in range(2):
        for d in range(n):
            if d > 0:
                @pl.when(h < d)
                def _():
                    rs_copy(arr, 0, d).wait_send()
            if d < n - 1:
                @pl.when(h > d)
                def _():
                    rs_copy(arr, 1, d).wait_send()


def on_device(n, nr, nc, tokens, valid, gain, w_qkv, w_proj, rel_table, cotangent):
    part_rows, ncol, width = tokens.shape
    tile_rows = part_rows * n
    part = part_rows * ncol
    heads = rel_table.shape[1]
    group = heads * HD
    pairs = heads // 2
    pos = WIN * WIN
    ucols = ncol // SHIFT

    row_lab = region(
        lax.axis_index("row") * tile_rows + jnp.arange(tile_rows, dtype=jnp.int32), tile_rows * nr
    )
    col_lab = region(lax.axis_index("col") * ncol + jnp.arange(ncol, dtype=jnp.int32), ncol * nc)
    labels = 3 * row_lab[:, None] + col_lab[None, :]

    def to_pairs(block):
        block = block.reshape(tile_rows // WIN, 2, SHIFT, ncol // WIN, 2, SHIFT)
        return block.transpose(0, 3, 1, 4, 2, 5).reshape(-1, 2 * pos)

    lab = to_pairs(labels) + 16 * (jnp.arange(2 * pos, dtype=jnp.int32) // pos)[None]
    val = to_pairs(valid)
    allowed = (lab[:, :, None] == lab[:, None, :]) & (
        (val[:, None, :] == 1) | jnp.eye(2 * pos, dtype=bool)[None]
    )
    mask = jnp.where(allowed, 0.0, -1e30).astype(F32)
    onehot = offsets()
    bias = jnp.dot(onehot, rel_table, precision=HIGH).reshape(pos, pos, heads).transpose(2, 0, 1)
    bias = jnp.broadcast_to(
        bias.reshape(pairs, 2, 1, pos, 1, pos), (pairs, 2, 2, pos, 2, pos)
    ).reshape(pairs, 4 * pos, 2 * pos)

    scale = 1.0 / math.sqrt(tile_rows * ncol * nr * nc)
    direct = nr * nc <= 8
    if direct:
        plane = [(dr, dc) for dr in range(nr) for dc in range(nc) if (dr, dc) != (0, 0)]
    else:
        six = [(1, 0), (nr - 1, 0), (0, 1), (0, nc - 1), (1, 1), (nr - 1, nc - 1)]
        plane = sorted(set(six))
    count = len(plane)
    piece = width // (nr * nc)
    vmem = pl.BlockSpec(memory_space=pltpu.VMEM)
    dma = pltpu.SemaphoreType.DMA
    mixed, token_gradient, wsum, tall = pl.pallas_call(
        functools.partial(kernel, (n, nr, nc, tuple(plane), direct, ncol, scale)),
        out_shape=(
            jax.ShapeDtypeStruct((part, width), BF16),
            jax.ShapeDtypeStruct((part, width), BF16),
            jax.ShapeDtypeStruct((group, piece if direct else width), F32),
            jax.ShapeDtypeStruct((pairs, pos, 2 * HD), F32),
        ),
        in_specs=[vmem] * 7,
        out_specs=[vmem] * 4,
        scratch_shapes=[
            pltpu.VMEM((part, width), F32),
            pltpu.VMEM((part, 1), F32),
            pltpu.VMEM((2, n, part, width), BF16),
            pltpu.VMEM((n + 1, ucols + 1, UNIT, 3 * group), BF16),
            pltpu.VMEM((n + 1, ucols + 1, UNIT, group), BF16),
            pltpu.VMEM((n + 1, ucols + 1, UNIT, group), BF16),
            pltpu.VMEM((n + 1, ucols + 1, UNIT, 3 * group), BF16),
            pltpu.VMEM((n * ucols // 8, pairs, 4 * pos, 2 * pos), F32),
            pltpu.VMEM((2, n, part, width), BF16),
            pltpu.VMEM((2, 2, n, part, width), BF16),
            pltpu.VMEM((nr * nc, group, piece) if direct else (1, 16, 128), BF16),
            pltpu.VMEM((count, group, piece) if direct else (1, 16, 128), BF16),
            pltpu.VMEM((pairs, pos, 2 * HD), F32),
            pltpu.VMEM((count, pairs, pos, 2 * HD) if direct else (1, 16, 128), F32),
            pltpu.VMEM((pairs, 4 * pos, 2 * pos), F32),
            dma((2, 2, n)),
            dma((2, 2, n)),
            dma((2, n + 1)),
            dma((2, n + 1)),
            dma((2, n + 1)),
            dma((2, n + 1)),
            dma((2, 2, n)),
            dma((2, 2, n)),
            dma((2, count)),
            dma((2, count)),
        ],
        compiler_params=pltpu.CompilerParams(
            collective_id=0, has_side_effects=True, vmem_limit_bytes=48 * 1024 * 1024
        ),
    )(
        tokens.reshape(part, width),
        cotangent.reshape(part, width),
        gain[None],
        w_qkv.transpose(1, 0, 2),
        w_proj,
        bias,
        mask,
    )
    if not direct:
        wsum = lax.psum_scatter(wsum, ("row", "col"), scatter_dimension=1, tiled=True) * scale
        tall = lax.psum(tall, ("row", "col"))
    summed = tall.reshape(pairs, pos, 2, pos).transpose(1, 3, 0, 2).reshape(pos * pos, heads)
    table_grad = jnp.dot(onehot.T, summed, precision=HIGH) * (WIN * scale)
    return (
        mixed.reshape(part_rows, ncol, width),
        token_gradient.reshape(part_rows, ncol, width),
        wsum,
        table_grad,
    )


def solution(mesh):
    n, nr, nc = (mesh.shape[name] for name in ("head", "row", "col"))
    return jax.shard_map(
        functools.partial(on_device, n, nr, nc),
        mesh=mesh,
        in_specs=(
            P(("row", "head"), "col", None),
            P("row", "col"),
            P(),
            P(None, None, "head"),
            P("head", None),
            P(None, "head"),
            P(("row", "head"), "col", None),
        ),
        out_specs=(
            P(("row", "head"), "col", None),
            P(("row", "head"), "col", None),
            P("head", ("row", "col")),
            P(None, "head"),
        ),
        check_vma=False,
    )
```

time: 116 us -> 106 us (0.914)
  the two profiles are of different devices: /device:TPU:12 before, /device:TPU:0 now
where the time goes in v2:
time: 106 us
  Pallas kernels  94.2 us (89%)
  local copies, waits for them, and re-layouts  5.67 us (5%)
  matrix products  4.83 us (5%)
    pallas_call x1, Pallas kernels, on_device(): pl.pallas_call(functools.partial(kernel, (n, nr, nc, tuple(plane), direct...  94.2 us
    unnamed x19, local copies, waits for them, and re-layouts  3.28 us
    dot_general x1, matrix products, on_device(): jnp.dot(onehot, rel_table, precision=HIGH).reshape(pos, pos, heads)  2.82 us

profile of v2, /device:TPU:0, one launch (start us, length us, event | category | flops | bytes accessed | tf_op | source)
XLA Modules:
  0.0 106.0 jit_solution(13174843221344196358)
XLA Ops:
  0.7 0.1 add_add_fusion
  0.8 0.6 copy-done
  1.3 2.8 %fusion = f32[64,64,4]{1,2,0:T(4,128)S(1)} fusion(s32[64,64]{1,0:T(8,128)S(1)} %add_add_fusion, f32[225,4]{0,1:T(4,128)S(1)} %copy-done), kind=kOutput, calls=%fused_computation.2 | convolution fusion | flops 45158400 | bytes 85520 | tf_op jit(solution)/shard_map/dot_general | solution.py:487
  4.2 0.1 broadcast_in_dim.56
  4.3 0.3 reshape.346.bias_ref
  4.7 0.1 broadcast_add_fusion
  4.8 0.1 add.209
  5.0 0.1 eq.73
  5.1 0.1 eq.75
  5.2 0.1 and_select_fusion.mask_ref
  5.4 94.2 %shard_map.102 = (bf16[128,1024]{1,0:T(8,128)(2,1)S(1)}, bf16[128,1024]{1,0:T(8,128)(2,1)S(1)}, f32[256,128]{1,0:T(8,128)S(1)}, f32[2,64,128]{2,1,0:T(8,128)S(1)}) custom-call(bf16[128,1024]{1,0:T(8,128)(2,1)S(1)} %bitcast.22, bf16[128,1024]{1,0:T(8,128)(2,1)S(1)} %bitcast.23, f32[1,1024]{1,0:T(1,128)S(1)} %bitcast.26, bf16[3,1024,256]{2,1,0:T(8,128)(2,1)S(1)} %bitcast.21, ...), custom_call_target="tpu_custom_call" | custom-call | tf_op jit(solution)/shard_map/pallas_call | solution.py:503
  99.7 0.6 copy-done.5
  100.3 1.0 reshape.349
  101.3 0.1 reshape.350
  101.4 0.1 sub.104
  101.4 0.1 sub.115
  101.6 0.1 sub.117
  101.6 0.1 sub.98
  101.7 0.1 sub.109
  101.8 0.1 sub.111
  101.9 2.0 %fusion.4 = f32[225,4]{0,1:T(4,128)} fusion(f32[4096,4]{0,1:T(4,128)S(1)} %reshape.350, s32[4096]{0:T(1024)S(1)} %add_add_fusion.1), kind=kOutput, calls=%fused_computation.6 | convolution fusion | flops 45159300 | bytes 85520 | tf_op jit(solution)/shard_map/dot_general | solution.py:556
  103.9 0.7 copy.23
  104.6 0.7 copy.24
  105.3 0.7 copy.25
  (27 shorter events, 0.2 us)
Async XLA Ops:
  0.6 0.7 copy-start
  0.6 4.3 %copy-start.7 = (s32[16,32]{1,0:T(8,128)S(1)}, s32[16,32]{1,0:T(8,128)}, u32[]{:S(2)}) copy-start(s32[16,32]{1,0:T(8,128)} %param.8) | copy-start | bytes 6148
  1.3 4.0 %copy-start.1 = (bf16[1024,3,256]{2,0,1:T(8,128)(2,1)S(1)}, bf16[1024,3,256]{2,0,1:T(8,128)(2,1)}, u32[]{:S(2)}) copy-start(bf16[1024,3,256]{2,0,1:T(8,128)(2,1)} %param.10) | copy-start | bytes 4718596
  1.3 4.0 %copy-start.2 = (bf16[256,1024]{1,0:T(8,128)(2,1)S(1)}, bf16[256,1024]{1,0:T(8,128)(2,1)}, u32[]{:S(2)}) copy-start(bf16[256,1024]{1,0:T(8,128)(2,1)} %wp_ref.1) | copy-start | bytes 1572868
  1.3 4.1 %copy-start.3 = (bf16[4,32,1024]{2,1,0:T(8,128)(2,1)S(1)}, bf16[4,32,1024]{2,1,0:T(8,128)(2,1)}, u32[]{:S(2)}) copy-start(bf16[4,32,1024]{2,1,0:T(8,128)(2,1)} %param.7) | copy-start | bytes 786436
  1.3 4.1 %copy-start.4 = (bf16[4,32,1024]{2,1,0:T(8,128)(2,1)S(1)}, bf16[4,32,1024]{2,1,0:T(8,128)(2,1)}, u32[]{:S(2)}) copy-start(bf16[4,32,1024]{2,1,0:T(8,128)(2,1)} %param.13) | copy-start | bytes 786436
  1.3 4.1 %copy-start.6 = (f32[1024]{0:T(1024)S(1)}, f32[1024]{0:T(1024)}, u32[]{:S(2)}) copy-start(f32[1024]{0:T(1024)} %param.9) | copy-start | bytes 12292
  99.6 0.6 copy-start.5

commit v3 on v2

--- a/solution.py
+++ b/solution.py
@@ -109,35 +109,40 @@
             return (h < n - 1) & (h >= t)
         return (h > 0) & (h < n - t)
 
-    def receives(way, t):
-        return h > t if way == 0 else h < n - 1 - t
-
-    def ag_send_step(arr, way, t):
-        @pl.when(sends(way, t))
+    short = jnp.minimum(h, n - 1 - h)
+
+    def arrival(k):
+        paired = k <= 2 * short
+        way = jnp.where(paired, lax.rem(k - 1, 2), jnp.where(2 * h > n - 1, 0, 1))
+        t = jnp.where(paired, (k - 1) // 2, k - 1 - short)
+        return way, t, 1 - 2 * way
+
+    def arrived_block(k):
+        way, t, step = arrival(k)
+        return jnp.where(k == 0, h, h - step * (t + 1))
+
+    def can_send(way):
+        return jnp.where(way == 0, h < n - 1, h > 0)
+
+    def receive(arr, k):
+        way, t, step = arrival(k)
+        blk = h - step * (t + 1)
+        pltpu.make_async_remote_copy(
+            src_ref=gath.at[arr, blk], dst_ref=gath.at[arr, blk],
+            send_sem=ag_send.at[arr, way, t], recv_sem=ag_recv.at[arr, way, t],
+            device_id={"head": h - step}, device_id_type=MESH,
+        ).wait_recv()
+
+        @pl.when(can_send(way))
         def _():
-            ag_copy(arr, way, t, h - (1 - 2 * way) * t).start()
-
-    def ag_receive_step(arr, way, t):
-        @pl.when(receives(way, t))
-        def _():
-            step = 1 - 2 * way
-            pltpu.make_async_remote_copy(
-                src_ref=gath.at[arr, h - step * (t + 1)],
-                dst_ref=gath.at[arr, h - step * (t + 1)],
-                send_sem=ag_send.at[arr, way, t], recv_sem=ag_recv.at[arr, way, t],
-                device_id={"head": h - step}, device_id_type=MESH,
-            ).wait_recv()
-        if t + 1 < n - 1:
-            ag_send_step(arr, way, t + 1)
-
-    def cot_after(t):
-        @pl.when((h == t) & (h < n - 1))
-        def _():
-            ag_copy(COT, 0, 0, h).start()
-
-        @pl.when((h == n - 1 - t) & (h > 0))
-        def _():
-            ag_copy(COT, 1, 0, h).start()
+            ag_copy(arr, way, t + 1, blk).start()
+
+        if arr == NORM:
+            last = t + 1 == jnp.where(way == 0, h, n - 1 - h)
+
+            @pl.when(last & can_send(way))
+            def _():
+                ag_copy(COT, way, 0, h).start()
 
     def in_copy(kind, k):
         tile = (tile_q, tile_g)[kind]
@@ -169,25 +174,23 @@
                 if k == 0:
                     in_copy(kind, n).start()
 
-    def project_step(kind, t):
-        for way in range(2):
-            @pl.when(receives(way, t))
-            def _():
-                project(kind, h - (1 - 2 * way) * (t + 1))
-
     for way in range(2):
-        ag_send_step(NORM, way, 0)
-    cot_after(0)
-    project(0, h)
-    for t in range(n - 1):
-        for way in range(2):
-            ag_receive_step(NORM, way, t)
-        cot_after(t + 1)
-        project_step(0, t)
-    project(1, h)
-    for way in range(2):
-        ag_receive_step(COT, way, 0)
-    project_step(1, 0)
+        @pl.when(sends(way, 0))
+        def _():
+            ag_copy(NORM, way, 0, h).start()
+
+        @pl.when(h == (0, n - 1)[way])
+        def _():
+            ag_copy(COT, way, 0, h).start()
+
+    @pl.loop(0, n)
+    def _(k):
+        @pl.when(k > 0)
+        def _():
+            receive(NORM, k)
+
+        project(0, arrived_block(k))
+
     for k in range(n + 1):
         in_copy(0, k).wait_recv()
 
@@ -263,25 +266,29 @@
         )
 
     def windows(kind, step, between):
-        for i in range(n // 2 - 1, -1, -1):
-            for jp in range(pairs2 - 1, -1, -1):
-                step(i, jp)
-                if jp == pairs2 - 1:
-                    for k in (2 * i + 1, 2 * i + 2):
-                        out_copy(kind, k if k < n else n).start()
-            if i == n // 2 - 1:
+        @pl.loop(0, n // 2 * pairs2)
+        def _(count):
+            i = n // 2 - 1 - count // pairs2
+            jp = pairs2 - 1 - lax.rem(count, pairs2)
+            step(i, jp)
+            for i_at in range(n // 2):
+                @pl.when((i == i_at) & (jp == pairs2 - 1))
+                def _():
+                    out_copy(kind, 2 * i_at + 1).start()
+                    out_copy(kind, 2 * i_at + 2).start()
+
+            @pl.when((i == n // 2 - 1) & (jp == 0))
+            def _():
                 out_copy(kind, 0).start()
-            between(i)
-
-    def between_forward(i):
-        if i == n // 2 - 1:
-            for t in range(1, n - 2):
-                for way in range(2):
-                    ag_receive_step(COT, way, t)
+
+            between(count)
+
+    def between_forward(count):
+        @pl.when(count < n - 2)
+        def _():
+            receive(COT, count + 1)
 
     windows(0, forward, between_forward)
-    for t in range(1, n - 2):
-        project_step(1, t)
     for k in range(n + 1):
         out_copy(0, k).wait_recv()
 
@@ -304,12 +311,13 @@
             device_id={"head": h - step}, device_id_type=MESH,
         ).wait_recv()
 
-    order = []
-    for k in range(n // 2):
-        order += [n - 1 - k, k]
+    def order(k):
+        return jnp.where(lax.rem(k, 2) == 0, n - 1 - k // 2, k // 2)
 
     def rs_start(arr):
-        for d in order:
+        @pl.loop(0, n)
+        def _(k):
+            d = order(k)
             if arr == 0:
                 term = dot(block(back_a, d), wp_ref[...], NN)
             else:
@@ -318,29 +326,24 @@
                     dot(grads[:, s * group : (s + 1) * group], wq_ref[s], NT) for s in range(3)
                 )
             terms[arr, d] = term.astype(BF16)
-            if d > 0:
-                @pl.when(h == 0)
-                def _():
-                    rs_copy(arr, 0, d).start()
-            if d < n - 1:
-                @pl.when(h == n - 1)
-                def _():
-                    rs_copy(arr, 1, d).start()
-
-    def pass_on(arr, way, d):
-        rs_arrived(arr, way, d)
-        terms[arr, d] = (terms[arr, d].astype(F32) + recv[arr, way, d].astype(F32)).astype(BF16)
-        rs_copy(arr, way, d).start()
-
-    def rs_transit(arr, d):
-        if d > 1:
-            @pl.when((h > 0) & (h < d))
+
+            @pl.when((h == 0) & (d > 0))
             def _():
-                pass_on(arr, 0, d)
-        if d < n - 2:
-            @pl.when((h > d) & (h < n - 1))
+                rs_copy(arr, 0, d).start()
+
+            @pl.when((h == n - 1) & (d < n - 1))
             def _():
-                pass_on(arr, 1, d)
+                rs_copy(arr, 1, d).start()
+
+    def rs_transit(arr, k):
+        d = order(k)
+
+        @pl.when(((h < d) & (h > 0)) | ((h > d) & (h < n - 1)))
+        def _():
+            way = jnp.where(h < d, 0, 1)
+            rs_arrived(arr, way, d)
+            terms[arr, d] = (terms[arr, d].astype(F32) + recv[arr, way, d].astype(F32)).astype(BF16)
+            rs_copy(arr, way, d).start()
 
     def total(arr):
         sides = [h > 0, h < n - 1]
@@ -357,18 +360,20 @@
         )
 
     rs_start(0)
-    for way in range(2):
-        ag_receive_step(COT, way, n - 2)
-    project_step(1, n - 2)
+
+    @pl.loop(0, n)
+    def _(k):
+        @pl.when(k == n - 1)
+        def _():
+            receive(COT, k)
+
+        project(1, arrived_block(k))
+
     for k in range(n + 1):
         in_copy(1, k).wait_recv()
 
-    def between_backward(i):
-        for d in order[: n // 2] if i == n // 2 - 1 else order[n // 2 :]:
-            rs_transit(0, d)
-
     tsum[...] = jnp.zeros_like(tsum)
-    windows(1, backward, between_backward)
+    windows(1, backward, functools.partial(rs_transit, 0))
 
     low = lax.broadcasted_iota(jnp.int32, (WIN * WIN, 2 * HD), 1) < HD
     for hp in range(heads2):
@@ -394,21 +399,30 @@
             device_id=there, device_id_type=MESH,
         )
 
-    attn = jnp.concatenate([block(back_a, d) for d in range(n)], 0)
-    wterm = dot(attn, gath[COT].reshape(n * part, width), TN)
+    wide = 2 * 128
+
+    @pl.loop(0, width // wide)
+    def _(j):
+        attn = back_a[pl.ds(0, n), pl.ds(0, ucols)].reshape(n * part, group)
+        cols = pl.ds(pl.multiple_of(j * wide, wide), wide)
+        wterm = dot(attn, gath[COT, :, :, cols].reshape(n * part, wide), TN)
+        if direct:
+            piece = width // (nr * nc)
+            for k in range(wide // piece):
+                wsend[wide // piece * j + k] = wterm[:, k * piece : (k + 1) * piece].astype(BF16)
+        else:
+            pg_ref[:, cols] = wterm
+
     if direct:
-        piece = width // (nr * nc)
-        for j in range(nr * nc):
-            wsend[j] = wterm[:, j * piece : (j + 1) * piece].astype(BF16)
         for o in range(len(plane)):
             for kind in range(2):
                 pl_copy(kind, o).start()
     else:
-        pg_ref[...] = wterm
         ts_ref[...] = tsend[...]
 
-    for d in order:
-        rs_transit(1, d)
+    @pl.loop(0, n)
+    def _(k):
+        rs_transit(1, k)
 
     mixed = dot(perm, tok_ref[...], NN) + total(0)
     mixed_ref[...] = dot(perm, mixed.astype(BF16), TN).astype(BF16)

time: 106 us -> 105 us (level)
  Pallas kernels: 94.2 us -> 93.1 us
    pallas_call x1, Pallas kernels: 94.2 us -> 93.1 us  [on_device(): pl.pallas_call(functools.partial(kernel, (n, nr, nc, tuple(plane), direct...]
where the time goes in v3:
time: 105 us
  Pallas kernels  93.1 us (89%)
  local copies, waits for them, and re-layouts  5.67 us (5%)
  matrix products  4.83 us (5%)
    pallas_call x1, Pallas kernels, on_device(): pl.pallas_call(functools.partial(kernel, (n, nr, nc, tuple(plane), direct...  93.1 us
    unnamed x19, local copies, waits for them, and re-layouts  3.28 us
    dot_general x1, matrix products, on_device(): jnp.dot(onehot, rel_table, precision=HIGH).reshape(pos, pos, heads)  2.82 us

profile of v3, /device:TPU:0, one launch (start us, length us, event | category | flops | bytes accessed | tf_op | source)
XLA Modules:
  0.0 104.8 jit_solution(2526062705898332109)
XLA Ops:
  0.7 0.1 add_add_fusion
  0.8 0.6 copy-done
  1.3 2.8 %fusion = f32[64,64,4]{1,2,0:T(4,128)S(1)} fusion(s32[64,64]{1,0:T(8,128)S(1)} %add_add_fusion, f32[225,4]{0,1:T(4,128)S(1)} %copy-done), kind=kOutput, calls=%fused_computation.2 | convolution fusion | flops 45158400 | bytes 85520 | tf_op jit(solution)/shard_map/dot_general | solution.py:501
  4.2 0.1 broadcast_in_dim.56
  4.3 0.3 reshape.346.bias_ref
  4.7 0.1 broadcast_add_fusion
  4.8 0.1 add.209
  5.0 0.1 eq.73
  5.1 0.1 eq.75
  5.2 0.1 and_select_fusion.mask_ref
  5.4 93.1 %shard_map.102 = (bf16[128,1024]{1,0:T(8,128)(2,1)S(1)}, bf16[128,1024]{1,0:T(8,128)(2,1)S(1)}, f32[256,128]{1,0:T(8,128)S(1)}, f32[2,64,128]{2,1,0:T(8,128)S(1)}) custom-call(bf16[128,1024]{1,0:T(8,128)(2,1)S(1)} %bitcast.22, bf16[128,1024]{1,0:T(8,128)(2,1)S(1)} %bitcast.23, f32[1,1024]{1,0:T(1,128)S(1)} %bitcast.26, bf16[3,1024,256]{2,1,0:T(8,128)(2,1)S(1)} %bitcast.21, ...), custom_call_target="tpu_custom_call" | custom-call | tf_op jit(solution)/shard_map/pallas_call | solution.py:517
  98.5 0.6 copy-done.5
  99.1 1.0 reshape.349
  100.1 0.1 reshape.350
  100.2 0.1 sub.104
  100.3 0.1 sub.115
  100.4 0.1 sub.117
  100.5 0.1 sub.98
  100.6 0.1 sub.109
  100.7 0.1 sub.111
  100.8 2.0 %fusion.4 = f32[225,4]{0,1:T(4,128)} fusion(f32[4096,4]{0,1:T(4,128)S(1)} %reshape.350, s32[4096]{0:T(1024)S(1)} %add_add_fusion.1), kind=kOutput, calls=%fused_computation.6 | convolution fusion | flops 45159300 | bytes 85520 | tf_op jit(solution)/shard_map/dot_general | solution.py:570
  102.8 0.7 copy.23
  103.5 0.7 copy.24
  104.2 0.7 copy.25
  (27 shorter events, 0.2 us)
Async XLA Ops:
  0.6 0.7 copy-start
  0.6 4.3 %copy-start.7 = (s32[16,32]{1,0:T(8,128)S(1)}, s32[16,32]{1,0:T(8,128)}, u32[]{:S(2)}) copy-start(s32[16,32]{1,0:T(8,128)} %param.8) | copy-start | bytes 6148
  1.3 4.0 %copy-start.1 = (bf16[1024,3,256]{2,0,1:T(8,128)(2,1)S(1)}, bf16[1024,3,256]{2,0,1:T(8,128)(2,1)}, u32[]{:S(2)}) copy-start(bf16[1024,3,256]{2,0,1:T(8,128)(2,1)} %param.10) | copy-start | bytes 4718596
  1.3 4.0 %copy-start.2 = (bf16[256,1024]{1,0:T(8,128)(2,1)S(1)}, bf16[256,1024]{1,0:T(8,128)(2,1)}, u32[]{:S(2)}) copy-start(bf16[256,1024]{1,0:T(8,128)(2,1)} %wp_ref.1) | copy-start | bytes 1572868
  1.3 4.1 %copy-start.3 = (bf16[4,32,1024]{2,1,0:T(8,128)(2,1)S(1)}, bf16[4,32,1024]{2,1,0:T(8,128)(2,1)}, u32[]{:S(2)}) copy-start(bf16[4,32,1024]{2,1,0:T(8,128)(2,1)} %param.7) | copy-start | bytes 786436
  1.3 4.1 %copy-start.4 = (bf16[4,32,1024]{2,1,0:T(8,128)(2,1)S(1)}, bf16[4,32,1024]{2,1,0:T(8,128)(2,1)}, u32[]{:S(2)}) copy-start(bf16[4,32,1024]{2,1,0:T(8,128)(2,1)} %param.13) | copy-start | bytes 786436
  1.3 4.1 %copy-start.6 = (f32[1024]{0:T(1024)S(1)}, f32[1024]{0:T(1024)}, u32[]{:S(2)}) copy-start(f32[1024]{0:T(1024)} %param.9) | copy-start | bytes 12292
  98.5 0.6 copy-start.5

commit v4 on v3

--- a/solution.py
+++ b/solution.py
@@ -312,7 +312,9 @@
         ).wait_recv()
 
     def order(k):
-        return jnp.where(lax.rem(k, 2) == 0, n - 1 - k // 2, k // 2)
+        far = n - 1 - k // 2
+        near = k // 2
+        return jnp.where((lax.rem(k, 2) == 0) == (2 * h < n - 1), far, near)
 
     def rs_start(arr):
         @pl.loop(0, n)
@@ -373,7 +375,12 @@
         in_copy(1, k).wait_recv()
 
     tsum[...] = jnp.zeros_like(tsum)
-    windows(1, backward, functools.partial(rs_transit, 0))
+    def between_backward(count):
+        @pl.when(count > 0)
+        def _():
+            rs_transit(0, count - 1)
+
+    windows(1, backward, between_backward)
 
     low = lax.broadcasted_iota(jnp.int32, (WIN * WIN, 2 * HD), 1) < HD
     for hp in range(heads2):

time: 105 us -> 89.7 us (0.85)
  Pallas kernels: 93.1 us -> 76.9 us
    pallas_call x1, Pallas kernels: 93.1 us -> 76.9 us  [on_device(): pl.pallas_call(functools.partial(kernel, (n, nr, nc, tuple(plane), direct...]
where the time goes in v4:
time: 89.7 us; the launch traced here: 88.6 us
  Pallas kernels  76.9 us (86%)
  local copies, waits for them, and re-layouts  5.67 us (6%)
  matrix products  4.83 us (5%)
    pallas_call x1, Pallas kernels, on_device(): pl.pallas_call(functools.partial(kernel, (n, nr, nc, tuple(plane), direct...  76.9 us
    unnamed x19, local copies, waits for them, and re-layouts  3.28 us
    dot_general x1, matrix products, on_device(): jnp.dot(onehot, rel_table, precision=HIGH).reshape(pos, pos, heads)  2.82 us
    dot_general x1, matrix products, on_device(): table_grad = jnp.dot(onehot.T, summed, precision=HIGH) * (WIN * scale)  2.01 us

profile of v4, /device:TPU:0, one launch (start us, length us, event | category | flops | bytes accessed | tf_op | source)
XLA Modules:
  0.0 88.6 jit_solution(17547139980200513407)
XLA Ops:
  0.7 0.1 add_add_fusion
  0.8 0.6 copy-done
  1.3 2.8 %fusion = f32[64,64,4]{1,2,0:T(4,128)S(1)} fusion(s32[64,64]{1,0:T(8,128)S(1)} %add_add_fusion, f32[225,4]{0,1:T(4,128)S(1)} %copy-done), kind=kOutput, calls=%fused_computation.2 | convolution fusion | flops 45158400 | bytes 85520 | tf_op jit(solution)/shard_map/dot_general | solution.py:508
  4.2 0.1 broadcast_in_dim.56
  4.3 0.3 reshape.346.bias_ref
  4.7 0.1 broadcast_add_fusion
  4.8 0.1 add.209
  5.0 0.1 eq.73
  5.1 0.1 eq.75
  5.2 0.1 and_select_fusion.mask_ref
  5.4 76.9 %shard_map.102 = (bf16[128,1024]{1,0:T(8,128)(2,1)S(1)}, bf16[128,1024]{1,0:T(8,128)(2,1)S(1)}, f32[256,128]{1,0:T(8,128)S(1)}, f32[2,64,128]{2,1,0:T(8,128)S(1)}) custom-call(bf16[128,1024]{1,0:T(8,128)(2,1)S(1)} %bitcast.22, bf16[128,1024]{1,0:T(8,128)(2,1)S(1)} %bitcast.23, f32[1,1024]{1,0:T(1,128)S(1)} %bitcast.26, bf16[3,1024,256]{2,1,0:T(8,128)(2,1)S(1)} %bitcast.21, ...), custom_call_target="tpu_custom_call" | custom-call | tf_op jit(solution)/shard_map/pallas_call | solution.py:524
  82.3 0.6 copy-done.5
  82.9 1.0 %reshape.349 = f32[2,64,2,64]{3,2,1,0:T(2,128)S(1)} reshape(f32[2,64,128]{2,1,0:T(8,128)} %copy-done.5) | data formatting | bytes 131072 | tf_op jit(solution)/shard_map/reshape | solution.py:576
  83.9 0.1 reshape.350
  84.0 0.1 sub.104
  84.1 0.1 sub.115
  84.2 0.1 sub.117
  84.3 0.1 sub.98
  84.4 0.1 sub.109
  84.5 0.1 sub.111
  84.6 2.0 %fusion.4 = f32[225,4]{0,1:T(4,128)} fusion(f32[4096,4]{0,1:T(4,128)S(1)} %reshape.350, s32[4096]{0:T(1024)S(1)} %add_add_fusion.1), kind=kOutput, calls=%fused_computation.6 | convolution fusion | flops 45159300 | bytes 85520 | tf_op jit(solution)/shard_map/dot_general | solution.py:577
  86.6 0.7 copy.23
  87.3 0.7 copy.24
  88.0 0.7 copy.25
  (27 shorter events, 0.2 us)
Async XLA Ops:
  0.6 0.7 copy-start
  0.6 4.3 %copy-start.7 = (s32[16,32]{1,0:T(8,128)S(1)}, s32[16,32]{1,0:T(8,128)}, u32[]{:S(2)}) copy-start(s32[16,32]{1,0:T(8,128)} %param.8) | copy-start | bytes 6148
  1.3 4.0 %copy-start.1 = (bf16[1024,3,256]{2,0,1:T(8,128)(2,1)S(1)}, bf16[1024,3,256]{2,0,1:T(8,128)(2,1)}, u32[]{:S(2)}) copy-start(bf16[1024,3,256]{2,0,1:T(8,128)(2,1)} %param.10) | copy-start | bytes 4718596
  1.3 4.0 %copy-start.2 = (bf16[256,1024]{1,0:T(8,128)(2,1)S(1)}, bf16[256,1024]{1,0:T(8,128)(2,1)}, u32[]{:S(2)}) copy-start(bf16[256,1024]{1,0:T(8,128)(2,1)} %wp_ref.1) | copy-start | bytes 1572868
  1.3 4.1 %copy-start.3 = (bf16[4,32,1024]{2,1,0:T(8,128)(2,1)S(1)}, bf16[4,32,1024]{2,1,0:T(8,128)(2,1)}, u32[]{:S(2)}) copy-start(bf16[4,32,1024]{2,1,0:T(8,128)(2,1)} %param.7) | copy-start | bytes 786436
  1.3 4.1 %copy-start.4 = (bf16[4,32,1024]{2,1,0:T(8,128)(2,1)S(1)}, bf16[4,32,1024]{2,1,0:T(8,128)(2,1)}, u32[]{:S(2)}) copy-start(bf16[4,32,1024]{2,1,0:T(8,128)(2,1)} %param.13) | copy-start | bytes 786436
  1.3 4.1 %copy-start.6 = (f32[1024]{0:T(1024)S(1)}, f32[1024]{0:T(1024)}, u32[]{:S(2)}) copy-start(f32[1024]{0:T(1024)} %param.9) | copy-start | bytes 12292
  82.3 0.6 copy-start.5

commit v5 on v4

--- a/solution.py
+++ b/solution.py
@@ -13,7 +13,6 @@
 SHIFT = 4
 UNIT = SHIFT * SHIFT
 EPS = 1e-05
-HIGH = lax.Precision.HIGHEST
 MESH = pl.DeviceIdType.MESH
 F32 = jnp.float32
 BF16 = jnp.bfloat16
@@ -32,32 +31,27 @@
     ).astype(jnp.int32)
 
 
-def window_places():
-    pos = jnp.arange(WIN * WIN, dtype=jnp.int32)
-    prow = pos // 32 * SHIFT + pos // SHIFT % SHIFT
-    pcol = pos // 16 % 2 * SHIFT + pos % SHIFT
-    return prow, pcol
-
-
-def offsets():
-    span = 2 * WIN - 1
-    prow, pcol = window_places()
-    index = (prow[:, None] - prow[None, :] + WIN - 1) * span + (
-        pcol[:, None] - pcol[None, :] + WIN - 1
-    )
-    table_ids = jnp.arange(span * span, dtype=jnp.int32)
-    return (
-        (index[:, :, None] == table_ids[None, None, :])
-        .astype(F32)
-        .reshape(WIN * WIN * WIN * WIN, span * span)
-    )
+def window_place(pos):
+    return pos // 32 * SHIFT + pos // SHIFT % SHIFT, pos // 16 % 2 * SHIFT + pos % SHIFT
+
+
+def parts_of(value):
+    high = value.astype(BF16)
+    rest = value - high.astype(F32)
+    mid = rest.astype(BF16)
+    return jnp.concatenate([high, mid, (rest - mid.astype(F32)).astype(BF16)], 0)
+
+
+def thirds(value):
+    rows = value.shape[0] // 3
+    return value[:rows] + value[rows : 2 * rows] + value[2 * rows :]
 
 
 def kernel(
     sizes,
-    tok_ref, cot_ref, gain_ref, wq_ref, wp_ref, bias_ref, mask_ref,
+    tok_ref, cot_ref, gain_ref, wq_ref, wp_ref, table_ref, mask_ref,
     mixed_ref, tg_ref, pg_ref, ts_ref,
-    xhat, rstd, gath, tile_q, tile_g, back_a, back_d, probs, terms, recv, wsend, wrecv, tsend, trecv, tsum,
+    xhat, rstd, gath, tile_q, tile_g, back_a, back_d, probs, terms, recv, wsend, wrecv, tsend, trecv, tsum, onehot, bias, flat,
     ag_send, ag_recv, in_send, in_recv, out_send, out_recv, rs_send, rs_recv,
     pl_send, pl_recv,
 ):
@@ -183,6 +177,27 @@
         def _():
             ag_copy(COT, way, 0, h).start()
 
+    heads = group // HD
+    span = 2 * WIN - 1
+    chunk = onehot.shape[2]
+    queries = chunk // (2 * HD)
+    rows, ids = table_ref.shape
+
+    @pl.loop(0, onehot.shape[0])
+    def _(j):
+        at_col = lax.broadcasted_iota(jnp.int32, (1, chunk), 1)
+        q_at = j * queries + at_col // (2 * HD)
+        k_at = at_col % HD
+        qr, qc = window_place(q_at)
+        kr, kc = window_place(k_at)
+        index = (qr - kr + WIN - 1) * span + qc - kc + WIN - 1
+        hot = lax.broadcasted_iota(jnp.int32, (ids, chunk), 0) == index
+        onehot[j] = jnp.where(hot, 1.0, 0.0).astype(BF16)
+        out = thirds(dot(parts_of(table_ref[...]), onehot[j], NN))
+        for k in range(heads):
+            for q in range(queries):
+                bias[k, pl.ds(j * queries + q, 1), :] = out[k : k + 1, q * 2 * HD : (q + 1) * 2 * HD]
+
     @pl.loop(0, n)
     def _(k):
         @pl.when(k > 0)
@@ -232,7 +247,8 @@
             base = hp * 2 * HD
             q, k, v = [load(tile_q, i, jp, base + s * group) for s in range(3)]
             m = mask_ref[pairs2 * i + jp]
-            s = dot(both(q), k, NT) * scale + bias_ref[hp] + jnp.concatenate([m, m], 0)
+            b = [bias[2 * hp], bias[2 * hp], bias[2 * hp + 1], bias[2 * hp + 1]]
+            s = dot(both(q), k, NT) * scale + jnp.concatenate(b, 0) + jnp.concatenate([m, m], 0)
             e = jnp.exp(s - jnp.max(s, -1, keepdims=True))
             p = e / jnp.sum(e, -1, keepdims=True)
             probs[pairs2 * i + jp, hp] = p
@@ -382,14 +398,6 @@
 
     windows(1, backward, between_backward)
 
-    low = lax.broadcasted_iota(jnp.int32, (WIN * WIN, 2 * HD), 1) < HD
-    for hp in range(heads2):
-        folds = []
-        for k in range(2):
-            f = tsum[hp, k * half : k * half + HD] + tsum[hp, k * half + HD : (k + 1) * half]
-            folds.append(f + pltpu.roll(f, HD, 1))
-        tsend[hp] = jnp.where(low, folds[0], folds[1])
-
     for k in range(n + 1):
         out_copy(1, k).wait_recv()
     rs_start(1)
@@ -422,12 +430,29 @@
 
     if direct:
         for o in range(len(plane)):
-            for kind in range(2):
-                pl_copy(kind, o).start()
+            pl_copy(0, o).start()
+    rs_transit(1, 0)
+
+    for k in range(heads):
+        hp, at_row = k // 2, k % 2 * half
+        bias[k] = tsum[hp, at_row : at_row + HD] + tsum[hp, at_row + HD : at_row + half]
+    flat[...] = jnp.zeros_like(flat)
+    tsend[...] = jnp.zeros_like(tsend)
+
+    @pl.loop(0, onehot.shape[0])
+    def _(j):
+        for k in range(heads):
+            for q in range(queries):
+                flat[k : k + 1, q * 2 * HD : (q + 1) * 2 * HD] = bias[k, pl.ds(j * queries + q, 1), :]
+        tsend[...] += thirds(dot(parts_of(flat[...]), onehot[j], NT))
+
+    if direct:
+        for o in range(len(plane)):
+            pl_copy(1, o).start()
     else:
         ts_ref[...] = tsend[...]
 
-    @pl.loop(0, n)
+    @pl.loop(1, n - 1)
     def _(k):
         rs_transit(1, k)
 
@@ -504,12 +529,8 @@
         (val[:, None, :] == 1) | jnp.eye(2 * pos, dtype=bool)[None]
     )
     mask = jnp.where(allowed, 0.0, -1e30).astype(F32)
-    onehot = offsets()
-    bias = jnp.dot(onehot, rel_table, precision=HIGH).reshape(pos, pos, heads).transpose(2, 0, 1)
-    bias = jnp.broadcast_to(
-        bias.reshape(pairs, 2, 1, pos, 1, pos), (pairs, 2, 2, pos, 2, pos)
-    ).reshape(pairs, 4 * pos, 2 * pos)
-
+    rows, ids = -(-heads // 16) * 16, 256
+    table = jnp.pad(rel_table.T, ((0, rows - heads), (0, ids - rel_table.shape[0])))
     scale = 1.0 / math.sqrt(tile_rows * ncol * nr * nc)
     direct = nr * nc <= 8
     if direct:
@@ -527,7 +548,7 @@
             jax.ShapeDtypeStruct((part, width), BF16),
             jax.ShapeDtypeStruct((part, width), BF16),
             jax.ShapeDtypeStruct((group, piece if direct else width), F32),
-            jax.ShapeDtypeStruct((pairs, pos, 2 * HD), F32),
+            jax.ShapeDtypeStruct((rows, ids), F32),
         ),
         in_specs=[vmem] * 7,
         out_specs=[vmem] * 4,
@@ -544,9 +565,12 @@
             pltpu.VMEM((2, 2, n, part, width), BF16),
             pltpu.VMEM((nr * nc, group, piece) if direct else (1, 16, 128), BF16),
             pltpu.VMEM((count, group, piece) if direct else (1, 16, 128), BF16),
-            pltpu.VMEM((pairs, pos, 2 * HD), F32),
-            pltpu.VMEM((count, pairs, pos, 2 * HD) if direct else (1, 16, 128), F32),
+            pltpu.VMEM((rows, ids), F32),
+            pltpu.VMEM((count, rows, ids) if direct else (1, 16, 128), F32),
             pltpu.VMEM((pairs, 4 * pos, 2 * pos), F32),
+            pltpu.VMEM((pos // 4, ids, 8 * HD), BF16),
+            pltpu.VMEM((heads, pos, 2 * HD), F32),
+            pltpu.VMEM((rows, 8 * HD), F32),
             dma((2, 2, n)),
             dma((2, 2, n)),
             dma((2, n + 1)),
@@ -567,14 +591,13 @@
         gain[None],
         w_qkv.transpose(1, 0, 2),
         w_proj,
-        bias,
+        table,
         mask,
     )
     if not direct:
         wsum = lax.psum_scatter(wsum, ("row", "col"), scatter_dimension=1, tiled=True) * scale
         tall = lax.psum(tall, ("row", "col"))
-    summed = tall.reshape(pairs, pos, 2, pos).transpose(1, 3, 0, 2).reshape(pos * pos, heads)
-    table_grad = jnp.dot(onehot.T, summed, precision=HIGH) * (WIN * scale)
+    table_grad = tall[:heads, : rel_table.shape[0]].T * (WIN * scale)
     return (
         mixed.reshape(part_rows, ncol, width),
         token_gradient.reshape(part_rows, ncol, width),

time: 89.7 us -> 88.4 us (0.986)
  matrix products: 4.83 us -> 0 us
  local copies, waits for them, and re-layouts: 5.67 us -> 8.13 us
  other arithmetic: 0.37 us -> 1.56 us
    dot_general x2 -> x0, matrix products: 4.83 us -> none  [the longest x1 2.82 us: on_device(): jnp.dot(onehot, rel_table, precision=HIGH).reshape(pos, pos, heads)]
    unnamed x19 -> x13, local copies, waits for them, and re-layouts: 3.28 us -> 7.09 us
    reshape x4 -> x0, local copies, waits for them, and re-layouts: 1.38 us -> none  [the longest x3 1.08 us: on_device(): tall.reshape(pairs, pos, 2, pos).transpose(1, 3, 0, 2)]
where the time goes in v5:
time: 88.4 us; the launch traced here: 87.3 us
  Pallas kernels  76.9 us (87%)
  local copies, waits for them, and re-layouts  8.13 us (9%)
  other arithmetic  1.56 us (2%)
    pallas_call x1, Pallas kernels, on_device(): pl.pallas_call(functools.partial(kernel, (n, nr, nc, tuple(plane), direct...  76.9 us
    unnamed x13, local copies, waits for them, and re-layouts  7.09 us

profile of v5, /device:TPU:0, one launch (start us, length us, event | category | flops | bytes accessed | tf_op | source)
XLA Modules:
  0.0 87.3 jit_solution(6597570575433949874)
XLA Ops:
  0.7 0.7 broadcast_compare_fusion
  1.4 0.7 pad.4.table_ref
  2.1 0.1 eq.45
  2.2 0.1 eq.47
  2.3 0.1 broadcast_add_fusion
  2.4 0.1 add.78
  2.6 0.1 and_select_fusion.mask_ref
  2.7 0.0 copy-start
  2.7 1.4 %copy-done = bf16[1024,3,256]{2,0,1:T(8,128)(2,1)S(1)} copy-done((bf16[1024,3,256]{2,0,1:T(8,128)(2,1)S(1)}, bf16[1024,3,256]{2,0,1:T(8,128)(2,1)}, u32[]{:S(2)}) %copy-start) | copy-done | bytes 1572888
  4.1 0.0 copy-start.1
  4.1 1.0 %copy-done.1 = bf16[256,1024]{1,0:T(8,128)(2,1)S(1)} copy-done((bf16[256,1024]{1,0:T(8,128)(2,1)S(1)}, bf16[256,1024]{1,0:T(8,128)(2,1)}, u32[]{:S(2)}) %copy-start.1) | copy-done | bytes 524312
  5.2 0.0 copy-start.2
  5.2 0.9 %copy-done.2 = bf16[4,32,1024]{2,1,0:T(8,128)(2,1)S(1)} copy-done((bf16[4,32,1024]{2,1,0:T(8,128)(2,1)S(1)}, bf16[4,32,1024]{2,1,0:T(8,128)(2,1)}, u32[]{:S(2)}) %copy-start.2) | copy-done | bytes 262168
  6.1 0.0 copy-start.3
  6.1 0.9 %copy-done.3 = bf16[4,32,1024]{2,1,0:T(8,128)(2,1)S(1)} copy-done((bf16[4,32,1024]{2,1,0:T(8,128)(2,1)S(1)}, bf16[4,32,1024]{2,1,0:T(8,128)(2,1)}, u32[]{:S(2)}) %copy-start.3) | copy-done | bytes 262168
  7.1 0.0 copy-start.4
  7.1 0.7 copy-done.4
  7.7 76.9 %shard_map.102 = (bf16[128,1024]{1,0:T(8,128)(2,1)S(1)}, bf16[128,1024]{1,0:T(8,128)(2,1)S(1)}, f32[256,128]{1,0:T(8,128)S(1)}, f32[16,256]{1,0:T(8,128)S(1)}) custom-call(bf16[128,1024]{1,0:T(8,128)(2,1)S(1)} %bitcast.13, bf16[128,1024]{1,0:T(8,128)(2,1)S(1)} %bitcast.14, f32[1,1024]{1,0:T(1,128)S(1)} %bitcast.15, bf16[3,1024,256]{2,1,0:T(8,128)(2,1)S(1)} %bitcast.10, ...), custom_call_target="tpu_custom_call" | custom-call | tf_op jit(solution)/shard_map/pallas_call | solution.py:545
  84.6 0.6 multiply_bitcast_fusion
  85.2 0.7 copy.16
  85.9 0.7 copy.17
  86.6 0.7 copy.18
  (6 shorter events, 0.1 us)
Async XLA Ops:
  2.7 1.4 %copy-start = (bf16[1024,3,256]{2,0,1:T(8,128)(2,1)S(1)}, bf16[1024,3,256]{2,0,1:T(8,128)(2,1)}, u32[]{:S(2)}) copy-start(bf16[1024,3,256]{2,0,1:T(8,128)(2,1)} %param.10) | copy-start | bytes 4718596
  4.1 1.0 %copy-start.1 = (bf16[256,1024]{1,0:T(8,128)(2,1)S(1)}, bf16[256,1024]{1,0:T(8,128)(2,1)}, u32[]{:S(2)}) copy-start(bf16[256,1024]{1,0:T(8,128)(2,1)} %wp_ref.1) | copy-start | bytes 1572868
  5.2 0.9 %copy-start.2 = (bf16[4,32,1024]{2,1,0:T(8,128)(2,1)S(1)}, bf16[4,32,1024]{2,1,0:T(8,128)(2,1)}, u32[]{:S(2)}) copy-start(bf16[4,32,1024]{2,1,0:T(8,128)(2,1)} %param.7) | copy-start | bytes 786436
  6.1 0.9 %copy-start.3 = (bf16[4,32,1024]{2,1,0:T(8,128)(2,1)S(1)}, bf16[4,32,1024]{2,1,0:T(8,128)(2,1)}, u32[]{:S(2)}) copy-start(bf16[4,32,1024]{2,1,0:T(8,128)(2,1)} %param.13) | copy-start | bytes 786436
  7.1 0.7 copy-start.4

commit v6 on v5

--- a/solution.py
+++ b/solution.py
@@ -49,9 +49,10 @@
 
 def kernel(
     sizes,
-    tok_ref, cot_ref, gain_ref, wq_ref, wp_ref, table_ref, mask_ref,
+    tok_hbm, cot_hbm, gain_ref, wq_hbm, wp_hbm, table_ref, valid_ref,
     mixed_ref, tg_ref, pg_ref, ts_ref,
     xhat, rstd, gath, tile_q, tile_g, back_a, back_d, probs, terms, recv, wsend, wrecv, tsend, trecv, tsum, onehot, bias, flat,
+    tok_ref, cot_ref, wq_ref, wp_ref, load_sem,
     ag_send, ag_recv, in_send, in_recv, out_send, out_recv, rs_send, rs_recv,
     pl_send, pl_recv,
 ):
@@ -67,6 +68,14 @@
     def at(dr, dc):
         return {"row": lax.rem(r + dr % nr, nr), "col": lax.rem(c + dc % nc, nc)}
 
+    sources = (tok_hbm, cot_hbm, wq_hbm, wp_hbm)
+    targets = (tok_ref, cot_ref, wq_ref, wp_ref)
+    loads = [
+        pltpu.make_async_copy(src, dst, load_sem.at[k])
+        for k, (src, dst) in enumerate(zip(sources, targets))
+    ]
+    for copy in loads:
+        copy.start()
     barrier = pltpu.get_barrier_semaphore()
     for dr, dc in plane:
         pl.semaphore_signal(barrier, inc=1, device_id=at(dr, dc), device_id_type=MESH)
@@ -80,6 +89,7 @@
     wanted = unit_at // SHIFT % SHIFT * ncol + unit_at // UNIT * SHIFT + unit_at % SHIFT
     perm = jnp.where(wanted == patch_at, 1.0, 0.0).astype(BF16)
 
+    loads[0].wait()
     x = dot(perm, tok_ref[...], NN)
     cen = x - jnp.mean(x, -1, keepdims=True)
     inv = lax.rsqrt(jnp.mean(cen * cen, -1, keepdims=True) + EPS)
@@ -87,6 +97,7 @@
     xhat[...] = std
     rstd[...] = inv
     gath[NORM, h] = (std * gain_ref[...]).astype(BF16)
+    loads[1].wait()
     gath[COT, h] = dot(perm, cot_ref[...], NN).astype(BF16)
     pl.semaphore_wait(barrier, len(plane) + 2)
 
@@ -198,6 +209,9 @@
             for q in range(queries):
                 bias[k, pl.ds(j * queries + q, 1), :] = out[k : k + 1, q * 2 * HD : (q + 1) * 2 * HD]
 
+    loads[2].wait()
+    loads[3].wait()
+
     @pl.loop(0, n)
     def _(k):
         @pl.when(k > 0)
@@ -242,11 +256,25 @@
     def chosen(value):
         return jnp.where(first, value[:half], value[half:])
 
+    def labels(i, jp, pos):
+        window = pos // (WIN * WIN)
+        prow, pcol = window_place(pos % (WIN * WIN))
+        row = region((r * (n // 2) + i) * WIN + prow, nr * n * SHIFT)
+        col = region(c * ncol + (2 * jp + window) * WIN + pcol, nc * ncol)
+        return 16 * window + 3 * row + col
+
+    def mask_of(i, jp):
+        q_at = lax.broadcasted_iota(jnp.int32, (half, 1), 0)
+        k_at = lax.broadcasted_iota(jnp.int32, (1, half), 1)
+        same = labels(i, jp, q_at) == labels(i, jp, k_at)
+        kept = (valid_ref[pl.ds(pairs2 * i + jp, 1), :] == 1) | (q_at == k_at)
+        return jnp.where(same & kept, 0.0, -1e30)
+
     def forward(i, jp):
+        m = mask_of(i, jp)
         for hp in range(heads2):
             base = hp * 2 * HD
             q, k, v = [load(tile_q, i, jp, base + s * group) for s in range(3)]
-            m = mask_ref[pairs2 * i + jp]
             b = [bias[2 * hp], bias[2 * hp], bias[2 * hp + 1], bias[2 * hp + 1]]
             s = dot(both(q), k, NT) * scale + jnp.concatenate(b, 0) + jnp.concatenate([m, m], 0)
             e = jnp.exp(s - jnp.max(s, -1, keepdims=True))
@@ -513,22 +541,10 @@
     pos = WIN * WIN
     ucols = ncol // SHIFT
 
-    row_lab = region(
-        lax.axis_index("row") * tile_rows + jnp.arange(tile_rows, dtype=jnp.int32), tile_rows * nr
-    )
-    col_lab = region(lax.axis_index("col") * ncol + jnp.arange(ncol, dtype=jnp.int32), ncol * nc)
-    labels = 3 * row_lab[:, None] + col_lab[None, :]
-
     def to_pairs(block):
         block = block.reshape(tile_rows // WIN, 2, SHIFT, ncol // WIN, 2, SHIFT)
         return block.transpose(0, 3, 1, 4, 2, 5).reshape(-1, 2 * pos)
 
-    lab = to_pairs(labels) + 16 * (jnp.arange(2 * pos, dtype=jnp.int32) // pos)[None]
-    val = to_pairs(valid)
-    allowed = (lab[:, :, None] == lab[:, None, :]) & (
-        (val[:, None, :] == 1) | jnp.eye(2 * pos, dtype=bool)[None]
-    )
-    mask = jnp.where(allowed, 0.0, -1e30).astype(F32)
     rows, ids = -(-heads // 16) * 16, 256
     table = jnp.pad(rel_table.T, ((0, rows - heads), (0, ids - rel_table.shape[0])))
     scale = 1.0 / math.sqrt(tile_rows * ncol * nr * nc)
@@ -541,6 +557,7 @@
     count = len(plane)
     piece = width // (nr * nc)
     vmem = pl.BlockSpec(memory_space=pltpu.VMEM)
+    hbm = pl.BlockSpec(memory_space=pltpu.HBM)
     dma = pltpu.SemaphoreType.DMA
     mixed, token_gradient, wsum, tall = pl.pallas_call(
         functools.partial(kernel, (n, nr, nc, tuple(plane), direct, ncol, scale)),
@@ -550,7 +567,7 @@
             jax.ShapeDtypeStruct((group, piece if direct else width), F32),
             jax.ShapeDtypeStruct((rows, ids), F32),
         ),
-        in_specs=[vmem] * 7,
+        in_specs=[hbm, hbm, vmem, hbm, hbm, vmem, vmem],
         out_specs=[vmem] * 4,
         scratch_shapes=[
             pltpu.VMEM((part, width), F32),
@@ -571,6 +588,11 @@
             pltpu.VMEM((pos // 4, ids, 8 * HD), BF16),
             pltpu.VMEM((heads, pos, 2 * HD), F32),
             pltpu.VMEM((rows, 8 * HD), F32),
+            pltpu.VMEM((part, width), BF16),
+            pltpu.VMEM((part, width), BF16),
+            pltpu.VMEM((3, width, group), BF16),
+            pltpu.VMEM((group, width), BF16),
+            dma((4,)),
             dma((2, 2, n)),
             dma((2, 2, n)),
             dma((2, n + 1)),
@@ -583,7 +605,7 @@
             dma((2, count)),
         ],
         compiler_params=pltpu.CompilerParams(
-            collective_id=0, has_side_effects=True, vmem_limit_bytes=48 * 1024 * 1024
+            collective_id=0, has_side_effects=True, vmem_limit_bytes=60 * 1024 * 1024
         ),
     )(
         tokens.reshape(part, width),
@@ -592,7 +614,7 @@
         w_qkv.transpose(1, 0, 2),
         w_proj,
         table,
-        mask,
+        to_pairs(valid),
     )
     if not direct:
         wsum = lax.psum_scatter(wsum, ("row", "col"), scatter_dimension=1, tiled=True) * scale

time: 88.4 us -> 89.4 us (1.011)
  Pallas kernels: 76.9 us -> 78.5 us
    unnamed x13 -> x3, local copies, waits for them, and re-layouts: 7.09 us -> 4.9 us
    pallas_call x1, Pallas kernels: 76.9 us -> 78.5 us  [on_device(): pl.pallas_call(functools.partial(kernel, (n, nr, nc, tuple(plane), direct...]
    reshape x0 -> x3, local copies, waits for them, and re-layouts: none -> 1.54 us  [the longest x2 0.84 us: to_pairs(): block = block.reshape(tile_rows // WIN, 2, SHIFT, ncol // WIN, 2, SHIFT)]
where the time goes in v6:
time: 89.4 us; the launch traced here: 88.2 us
  Pallas kernels  78.5 us (88%)
  local copies, waits for them, and re-layouts  7.74 us (9%)
  other arithmetic  1.29 us (1%)
    pallas_call x1, Pallas kernels, on_device(): pl.pallas_call(functools.partial(kernel, (n, nr, nc, tuple(plane), direct...  78.5 us
    unnamed x3, local copies, waits for them, and re-layouts  4.9 us

profile of v6, /device:TPU:0, one launch (start us, length us, event | category | flops | bytes accessed | tf_op | source)
XLA Modules:
  0.0 88.2 jit_solution(8902792476342396099)
XLA Ops:
  0.6 1.3 %pad.4.table_ref = f32[16,256]{1,0:T(8,128)} pad(f32[4,225]{1,0:T(4,128)} %bitcast.19, f32[]{:T(128)} %constant.1.clone.1), padding=0_12x0_31 | pad | bytes 19988 | tf_op jit(solution)/shard_map/jit(_pad)/pad | solution.py:549
  1.9 0.8 reshape.28
  2.8 0.7 reshape.29.valid_ref
  3.5 78.5 %shard_map.102 = (bf16[128,1024]{1,0:T(8,128)(2,1)}, bf16[128,1024]{1,0:T(8,128)(2,1)}, f32[256,128]{1,0:T(8,128)}, f32[16,256]{1,0:T(8,128)}) custom-call(bf16[128,1024]{1,0:T(8,128)(2,1)} %bitcast.13, bf16[128,1024]{1,0:T(8,128)(2,1)} %bitcast.14, f32[1,1024]{1,0:T(1,128)} %bitcast.18, bf16[3,1024,256]{2,1,0:T(8,128)(2,1)} %bitcast.12, ...), custom_call_target="tpu_custom_call" | custom-call | tf_op jit(solution)/shard_map/pallas_call | solution.py:562
  82.0 1.3 %multiply_bitcast_fusion = f32[225,4]{0,1:T(4,128)} fusion(f32[16,256]{1,0:T(8,128)} %get-tuple-element.11), kind=kLoop, calls=%fused_computation.1 | loop fusion | flops 900 | bytes 7200 | tf_op jit(solution)/shard_map/mul | solution.py:622
  83.3 1.7 %copy.17 = bf16[4,32,1024]{2,1,0:T(8,128)(2,1)} copy(bf16[4,32,1024]{2,1,0:T(8,128)(2,1)} %bitcast.16) | data formatting | bytes 524288
  85.0 1.7 %copy.18 = bf16[4,32,1024]{2,1,0:T(8,128)(2,1)} copy(bf16[4,32,1024]{2,1,0:T(8,128)(2,1)} %bitcast.15) | data formatting | bytes 524288
  86.7 1.6 %copy.19 = f32[256,128]{1,0:T(8,128)} copy(f32[256,128]{1,0:T(8,128)} %get-tuple-element.18) | data formatting | bytes 262144
  (1 shorter events, 0.0 us)

commit v7 on v6

--- a/solution.py
+++ b/solution.py
@@ -605,7 +605,7 @@
             dma((2, count)),
         ],
         compiler_params=pltpu.CompilerParams(
-            collective_id=0, has_side_effects=True, vmem_limit_bytes=60 * 1024 * 1024
+            collective_id=0, has_side_effects=True, vmem_limit_bytes=53 * 1024 * 1024
         ),
     )(
         tokens.reshape(part, width),

time: 89.4 us -> 84.6 us (0.946)
  local copies, waits for them, and re-layouts: 7.74 us -> 5.34 us
  Pallas kernels: 78.5 us -> 76.9 us
    pallas_call x1, Pallas kernels: 78.5 us -> 76.9 us  [on_device(): pl.pallas_call(functools.partial(kernel, (n, nr, nc, tuple(plane), direct...]
    unnamed x3 -> x7, local copies, waits for them, and re-layouts: 4.9 us -> 3.69 us
where the time goes in v7:
time: 84.6 us; the launch traced here: 83.5 us
  Pallas kernels  76.9 us (91%)
  local copies, waits for them, and re-layouts  5.34 us (6%)
    pallas_call x1, Pallas kernels, on_device(): pl.pallas_call(functools.partial(kernel, (n, nr, nc, tuple(plane), direct...  76.9 us
    unnamed x7, local copies, waits for them, and re-layouts  3.69 us

profile of v7, /device:TPU:0, one launch (start us, length us, event | category | flops | bytes accessed | tf_op | source)
XLA Modules:
  0.0 83.5 jit_solution(6452179594725198114)
XLA Ops:
  0.6 0.7 pad.4.table_ref
  1.3 0.8 reshape.28
  2.2 0.1 reshape.29.valid_ref
  2.3 0.0 copy-start
  2.3 0.9 %copy-done = bf16[4,32,1024]{2,1,0:T(8,128)(2,1)S(1)} copy-done((bf16[4,32,1024]{2,1,0:T(8,128)(2,1)S(1)}, bf16[4,32,1024]{2,1,0:T(8,128)(2,1)}, u32[]{:S(2)}) %copy-start) | copy-done | bytes 262168
  3.3 0.0 copy-start.1
  3.3 0.7 copy-done.1
  3.9 76.9 %shard_map.102 = (bf16[128,1024]{1,0:T(8,128)(2,1)S(1)}, bf16[128,1024]{1,0:T(8,128)(2,1)S(1)}, f32[256,128]{1,0:T(8,128)S(1)}, f32[16,256]{1,0:T(8,128)S(1)}) custom-call(bf16[128,1024]{1,0:T(8,128)(2,1)S(1)} %bitcast.12, bf16[128,1024]{1,0:T(8,128)(2,1)} %bitcast.17, f32[1,1024]{1,0:T(1,128)S(1)} %bitcast.15, bf16[3,1024,256]{2,1,0:T(8,128)(2,1)} %bitcast.16, ...), custom_call_target="tpu_custom_call" | custom-call | tf_op jit(solution)/shard_map/pallas_call | solution.py:562
  80.8 0.6 multiply_bitcast_fusion
  81.4 0.7 copy.17
  82.1 0.7 copy.18
  82.8 0.7 copy.19
  (1 shorter events, 0.0 us)
Async XLA Ops:
  2.3 1.0 %copy-start = (bf16[4,32,1024]{2,1,0:T(8,128)(2,1)S(1)}, bf16[4,32,1024]{2,1,0:T(8,128)(2,1)}, u32[]{:S(2)}) copy-start(bf16[4,32,1024]{2,1,0:T(8,128)(2,1)} %param.7) | copy-start | bytes 786436
  3.3 0.7 copy-start.1
